TPU v7x, 32 devices: a whole 2x2x4 slice. The times are simulated.
32 devices in a mesh: fsdp: 8 (over z, y), rep: 4 (over x, core).
Axes of the slice: x: 2, y: 2, z: 4, core: 2. Of those that a mesh axis runs over, the one named last changes fastest.
Arguments:
- anchors: float32 [3, 1024], P(None, ('fsdp', 'rep')), may hold values from -4 to 4
- directions: float32 [3, 1024], P(None, ('fsdp', 'rep')), may hold values from -4 to 4
- deltas: float32 [1024, 128], P(('fsdp', 'rep')), may hold values from 0.02 to 0.1
- foreground: int32 [1024, 128], P(('fsdp', 'rep')), may hold values from 0 to 1, as said below
- sdf_first_dir: bfloat16 [39, 256], P(None, ('fsdp', 'rep')), may hold values from -1 to 1
- sdf_first_gain: bfloat16 [256], P(('fsdp', 'rep')), may hold values from 0.5 to 2
- sdf_first_bias: bfloat16 [256], P(('fsdp', 'rep')), may hold values from -1.5 to 1.5
- sdf_mid_dir: bfloat16 [4, 256, 256], P(None, None, ('fsdp', 'rep')), may hold values from -0.375 to 0.375
- sdf_mid_gain: bfloat16 [4, 256], P(None, ('fsdp', 'rep')), may hold values from 0.5 to 2
- sdf_mid_bias: bfloat16 [4, 256], P(None, ('fsdp', 'rep')), may hold values from -1.5 to 1.5
- sdf_narrow_dir: bfloat16 [256, 217], P(('fsdp', 'rep')), may hold values from -0.375 to 0.375
- sdf_narrow_gain: bfloat16 [217], replicated, may hold values from 0.5 to 2
- sdf_narrow_bias: bfloat16 [217], replicated, may hold values from -1.5 to 1.5
- sdf_skip_dir: bfloat16 [256, 256], P(None, ('fsdp', 'rep')), may hold values from -0.375 to 0.375
- sdf_skip_gain: bfloat16 [256], P(('fsdp', 'rep')), may hold values from 0.5 to 2
- sdf_skip_bias: bfloat16 [256], P(('fsdp', 'rep')), may hold values from -1.5 to 1.5
- sdf_last_dir: bfloat16 [256, 257], P(('fsdp', 'rep')), may hold values from -0.375 to 0.375
- sdf_last_gain: bfloat16 [257], replicated, may hold values from 0.5 to 2
- sdf_last_bias: bfloat16 [257], replicated, may hold values from -1.5 to 1.5
- color_first_dir: bfloat16 [289, 256], P(None, ('fsdp', 'rep')), may hold values from -0.375 to 0.375
- color_first_gain: bfloat16 [256], P(('fsdp', 'rep')), may hold values from 0.5 to 2
- color_first_bias: bfloat16 [256], P(('fsdp', 'rep')), may hold values from -1.5 to 1.5
- color_mid_dir: bfloat16 [3, 256, 256], P(None, None, ('fsdp', 'rep')), may hold values from -0.375 to 0.375
- color_mid_gain: bfloat16 [3, 256], P(None, ('fsdp', 'rep')), may hold values from 0.5 to 2
- color_mid_bias: bfloat16 [3, 256], P(None, ('fsdp', 'rep')), may hold values from -1.5 to 1.5
- color_last_dir: bfloat16 [256, 3], P(('fsdp', 'rep')), may hold values from -0.375 to 0.375
- color_last_gain: bfloat16 [3], replicated, may hold values from 0.5 to 2
- color_last_bias: bfloat16 [3], replicated, may hold values from -1.5 to 1.5
- variance: float32 [1], replicated, may hold values from 0.05 to 0.15
- rgb_cotangent: float32 [3, 1024], P(None, ('fsdp', 'rep')), may hold values from -6 to 6
Outputs:
- rgb: float32 [3, 1024], P(None, ('fsdp', 'rep'))
- anchors_grad: float32 [3, 1024], P(None, ('fsdp', 'rep'))
- directions_grad: float32 [3, 1024], P(None, ('fsdp', 'rep'))
- deltas_grad: float32 [1024, 128], P(('fsdp', 'rep'))
- sdf_first_dir_grad: float32 [39, 256], P(None, ('fsdp', 'rep'))
- sdf_first_gain_grad: float32 [256], P(('fsdp', 'rep'))
- sdf_first_bias_grad: float32 [256], P(('fsdp', 'rep'))
- sdf_mid_dir_grad: float32 [4, 256, 256], P(None, None, ('fsdp', 'rep'))
- sdf_mid_gain_grad: float32 [4, 256], P(None, ('fsdp', 'rep'))
- sdf_mid_bias_grad: float32 [4, 256], P(None, ('fsdp', 'rep'))
- sdf_narrow_dir_grad: float32 [256, 217], P(('fsdp', 'rep'))
- sdf_narrow_gain_grad: float32 [217], replicated
- sdf_narrow_bias_grad: float32 [217], replicated
- sdf_skip_dir_grad: float32 [256, 256], P(None, ('fsdp', 'rep'))
- sdf_skip_gain_grad: float32 [256], P(('fsdp', 'rep'))
- sdf_skip_bias_grad: float32 [256], P(('fsdp', 'rep'))
- sdf_last_dir_grad: float32 [256, 257], P(('fsdp', 'rep'))
- sdf_last_gain_grad: float32 [257], replicated
- sdf_last_bias_grad: float32 [257], replicated
- color_first_dir_grad: float32 [289, 256], P(None, ('fsdp', 'rep'))
- color_first_gain_grad: float32 [256], P(('fsdp', 'rep'))
- color_first_bias_grad: float32 [256], P(('fsdp', 'rep'))
- color_mid_dir_grad: float32 [3, 256, 256], P(None, None, ('fsdp', 'rep'))
- color_mid_gain_grad: float32 [3, 256], P(None, ('fsdp', 'rep'))
- color_mid_bias_grad: float32 [3, 256], P(None, ('fsdp', 'rep'))
- color_last_dir_grad: float32 [256, 3], P(('fsdp', 'rep'))
- color_last_gain_grad: float32 [3], replicated
- color_last_bias_grad: float32 [3], replicated
- variance_grad: float32 [1], replicated
Inputs may be any that keep to these rules, and one draw needn't show every extreme that they name: The share of foreground samples differs from one device's 32 rays to another's; in every draw the rays of some device are foreground at every sample.
All inputs are finite; a program needn't handle non-finite values.
Results may differ from a plain program's by a relative error of at most 0.039.
The roundings to bfloat16 on the way count: a program that leaves them out, or rounds other values in their place, can miss the bound.
Values may be sent and summed in bfloat16 or wider, within the bound.
A program may use at most 320 MiB of HBM per device.

v0:
```python
import jax
import jax.numpy as jnp
from jax import lax
from jax.sharding import PartitionSpec as P

FREQ = 6
VFREQ = 4


eps_norm = 1e-06
near_plane = 0.1
root_half = 0.7071067811865476


def project(rows, weight, offset):
    return (
        jnp.dot(
            rows.astype(jnp.bfloat16),
            weight.astype(jnp.bfloat16),
            preferred_element_type=jnp.float32,
        )
        + offset
    )


def scaled(direction, column_gain):
    return direction * (column_gain * lax.rsqrt(jnp.sum(direction * direction, axis=0) + eps_norm))


def sharp(values):
    return jax.nn.softplus(2.0 * values) / 2.0


def encode(points, repeats):
    pieces = [points]
    for octave in range(repeats):
        pieces.append(jnp.sin(points * 2.0**octave))
        pieces.append(jnp.cos(points * 2.0**octave))
    return jnp.concatenate(pieces, axis=1)


def sdf_net(params, points):
    first_dir, first_gain, first_bias, mid_dir, mid_gain, mid_bias = params[0:6]
    narrow_dir, narrow_gain, narrow_bias, skip_dir, skip_gain, skip_bias = params[6:12]
    last_dir, last_gain, last_bias = params[12:15]
    encoded = encode(points, FREQ)
    hidden = sharp(project(encoded, scaled(first_dir, first_gain), first_bias))
    for section in range(2):
        hidden = sharp(
            project(hidden, scaled(mid_dir[section], mid_gain[section]), mid_bias[section])
        )
    hidden = sharp(project(hidden, scaled(narrow_dir, narrow_gain), narrow_bias))
    hidden = jnp.concatenate([hidden, encoded], axis=1) * root_half
    hidden = sharp(project(hidden, scaled(skip_dir, skip_gain), skip_bias))
    for section in range(2, 4):
        hidden = sharp(
            project(hidden, scaled(mid_dir[section], mid_gain[section]), mid_bias[section])
        )
    output = project(hidden, scaled(last_dir, last_gain), last_bias)
    return (output[:, 0], output[:, 1:])


def color_net(params, points, viewing, normal, features):
    first_dir, first_gain, first_bias, mid_dir, mid_gain, mid_bias = params[15:21]
    last_dir, last_gain, last_bias = params[21:24]
    joined = jnp.concatenate([points, encode(viewing, VFREQ), normal, features], axis=1)
    hidden = jax.nn.silu(project(joined, scaled(first_dir, first_gain), first_bias))
    for section in range(3):
        hidden = jax.nn.silu(
            project(hidden, scaled(mid_dir[section], mid_gain[section]), mid_bias[section])
        )
    return jax.nn.sigmoid(project(hidden, scaled(last_dir, last_gain), last_bias))


def render(params, anchors, directions, deltas, foreground):
    anchor_rows = anchors.T
    direction_rows = directions.T
    ray_count, sample_count = deltas.shape
    depths = near_plane + jnp.cumsum(deltas, axis=1) - 0.5 * deltas
    points = (anchor_rows[:, None, :] + depths[:, :, None] * direction_rows[:, None, :]).reshape(
        ray_count * sample_count, 3
    )
    viewing = jnp.broadcast_to(direction_rows[:, None, :], (ray_count, sample_count, 3)).reshape(
        ray_count * sample_count, 3
    )

    def sdf_total(moved):
        signed, features = sdf_net(params, moved)
        return (jnp.sum(signed), (signed, features))

    normal, (signed, features) = jax.grad(sdf_total, has_aux=True)(points)
    colors = color_net(params, points, viewing, normal, features).reshape(
        ray_count, sample_count, 3
    )
    cosine = jnp.sum(viewing * normal, axis=1)
    slope_term = -jax.nn.softplus(-10.0 * cosine) / 10.0
    halfway = slope_term * deltas.reshape(-1) * 0.5
    inverse_s = jnp.exp(10.0 * params[24][0])
    before = jax.nn.sigmoid((signed - halfway) * inverse_s)
    after = jax.nn.sigmoid((signed + halfway) * inverse_s)
    ratio = (before - after + 1e-05) / (before + 1e-05)
    opacity = (jax.nn.softplus(20.0 * ratio) - jax.nn.softplus(20.0 * (ratio - 1.0))) / 20.0
    opacity = foreground * opacity.reshape(ray_count, sample_count)
    survive = jnp.cumprod(1.0 - opacity + 1e-07, axis=1)
    through = jnp.concatenate([jnp.ones((ray_count, 1), jnp.float32), survive[:, :-1]], axis=1)
    contrib = opacity * through
    return jnp.sum(contrib[:, :, None] * colors, axis=1).T


def assemble(gathered, kept):
    return (
        gathered[0],
        gathered[1],
        gathered[2],
        gathered[3],
        gathered[4],
        gathered[5],
        gathered[6],
        kept[0],
        kept[1],
        gathered[7],
        gathered[8],
        gathered[9],
        gathered[10],
        kept[2],
        kept[3],
        gathered[11],
        gathered[12],
        gathered[13],
        gathered[14],
        gathered[15],
        gathered[16],
        gathered[17],
        kept[4],
        kept[5],
        kept[6],
    )


def widen(entries):
    return tuple((entry.astype(jnp.float32) for entry in entries))


def per_device(
    anchors,
    directions,
    deltas,
    foreground,
    sdf_first_dir,
    sdf_first_gain,
    sdf_first_bias,
    sdf_mid_dir,
    sdf_mid_gain,
    sdf_mid_bias,
    sdf_narrow_dir,
    sdf_narrow_gain,
    sdf_narrow_bias,
    sdf_skip_dir,
    sdf_skip_gain,
    sdf_skip_bias,
    sdf_last_dir,
    sdf_last_gain,
    sdf_last_bias,
    color_first_dir,
    color_first_gain,
    color_first_bias,
    color_mid_dir,
    color_mid_gain,
    color_mid_bias,
    color_last_dir,
    color_last_gain,
    color_last_bias,
    variance,
    rgb_cotangent,
):
    kept = widen(
        (
            sdf_narrow_gain,
            sdf_narrow_bias,
            sdf_last_gain,
            sdf_last_bias,
            color_last_gain,
            color_last_bias,
            variance,
        )
    )
    fore_float = foreground.astype(jnp.float32)
    gathered = (
        lax.all_gather(sdf_first_dir, ("fsdp", "rep"), axis=1, tiled=True),
        lax.all_gather(sdf_first_gain, ("fsdp", "rep"), axis=0, tiled=True),
        lax.all_gather(sdf_first_bias, ("fsdp", "rep"), axis=0, tiled=True),
        lax.all_gather(sdf_mid_dir, ("fsdp", "rep"), axis=2, tiled=True),
        lax.all_gather(sdf_mid_gain, ("fsdp", "rep"), axis=1, tiled=True),
        lax.all_gather(sdf_mid_bias, ("fsdp", "rep"), axis=1, tiled=True),
        lax.all_gather(sdf_narrow_dir, ("fsdp", "rep"), axis=0, tiled=True),
        lax.all_gather(sdf_skip_dir, ("fsdp", "rep"), axis=1, tiled=True),
        lax.all_gather(sdf_skip_gain, ("fsdp", "rep"), axis=0, tiled=True),
        lax.all_gather(sdf_skip_bias, ("fsdp", "rep"), axis=0, tiled=True),
        lax.all_gather(sdf_last_dir, ("fsdp", "rep"), axis=0, tiled=True),
        lax.all_gather(color_first_dir, ("fsdp", "rep"), axis=1, tiled=True),
        lax.all_gather(color_first_gain, ("fsdp", "rep"), axis=0, tiled=True),
        lax.all_gather(color_first_bias, ("fsdp", "rep"), axis=0, tiled=True),
        lax.all_gather(color_mid_dir, ("fsdp", "rep"), axis=2, tiled=True),
        lax.all_gather(color_mid_gain, ("fsdp", "rep"), axis=1, tiled=True),
        lax.all_gather(color_mid_bias, ("fsdp", "rep"), axis=1, tiled=True),
        lax.all_gather(color_last_dir, ("fsdp", "rep"), axis=0, tiled=True),
    )

    def whole(params, anchor_part, direction_part, delta_part):
        return render(params, anchor_part, direction_part, delta_part, fore_float)

    rgb = whole(assemble(widen(gathered), kept), anchors, directions, deltas)
    again = (
        lax.all_gather(sdf_first_dir, ("fsdp", "rep"), axis=1, tiled=True),
        lax.all_gather(sdf_first_gain, ("fsdp", "rep"), axis=0, tiled=True),
        lax.all_gather(sdf_first_bias, ("fsdp", "rep"), axis=0, tiled=True),
        lax.all_gather(sdf_mid_dir, ("fsdp", "rep"), axis=2, tiled=True),
        lax.all_gather(sdf_mid_gain, ("fsdp", "rep"), axis=1, tiled=True),
        lax.all_gather(sdf_mid_bias, ("fsdp", "rep"), axis=1, tiled=True),
        lax.all_gather(sdf_narrow_dir, ("fsdp", "rep"), axis=0, tiled=True),
        lax.all_gather(sdf_skip_dir, ("fsdp", "rep"), axis=1, tiled=True),
        lax.all_gather(sdf_skip_gain, ("fsdp", "rep"), axis=0, tiled=True),
        lax.all_gather(sdf_skip_bias, ("fsdp", "rep"), axis=0, tiled=True),
        lax.all_gather(sdf_last_dir, ("fsdp", "rep"), axis=0, tiled=True),
        lax.all_gather(color_first_dir, ("fsdp", "rep"), axis=1, tiled=True),
        lax.all_gather(color_first_gain, ("fsdp", "rep"), axis=0, tiled=True),
        lax.all_gather(color_first_bias, ("fsdp", "rep"), axis=0, tiled=True),
        lax.all_gather(color_mid_dir, ("fsdp", "rep"), axis=2, tiled=True),
        lax.all_gather(color_mid_gain, ("fsdp", "rep"), axis=1, tiled=True),
        lax.all_gather(color_mid_bias, ("fsdp", "rep"), axis=1, tiled=True),
        lax.all_gather(color_last_dir, ("fsdp", "rep"), axis=0, tiled=True),
    )
    unused, pullback = jax.vjp(whole, assemble(widen(again), kept), anchors, directions, deltas)
    grads, anchors_grad, directions_grad, deltas_grad = pullback(rgb_cotangent)
    shares = (
        lax.psum_scatter(grads[0], ("fsdp", "rep"), scatter_dimension=1, tiled=True),
        lax.psum_scatter(grads[1], ("fsdp", "rep"), scatter_dimension=0, tiled=True),
        lax.psum_scatter(grads[2], ("fsdp", "rep"), scatter_dimension=0, tiled=True),
        lax.psum_scatter(grads[3], ("fsdp", "rep"), scatter_dimension=2, tiled=True),
        lax.psum_scatter(grads[4], ("fsdp", "rep"), scatter_dimension=1, tiled=True),
        lax.psum_scatter(grads[5], ("fsdp", "rep"), scatter_dimension=1, tiled=True),
        lax.psum_scatter(grads[6], ("fsdp", "rep"), scatter_dimension=0, tiled=True),
        lax.psum_scatter(grads[9], ("fsdp", "rep"), scatter_dimension=1, tiled=True),
        lax.psum_scatter(grads[10], ("fsdp", "rep"), scatter_dimension=0, tiled=True),
        lax.psum_scatter(grads[11], ("fsdp", "rep"), scatter_dimension=0, tiled=True),
        lax.psum_scatter(grads[12], ("fsdp", "rep"), scatter_dimension=0, tiled=True),
        lax.psum_scatter(grads[15], ("fsdp", "rep"), scatter_dimension=1, tiled=True),
        lax.psum_scatter(grads[16], ("fsdp", "rep"), scatter_dimension=0, tiled=True),
        lax.psum_scatter(grads[17], ("fsdp", "rep"), scatter_dimension=0, tiled=True),
        lax.psum_scatter(grads[18], ("fsdp", "rep"), scatter_dimension=2, tiled=True),
        lax.psum_scatter(grads[19], ("fsdp", "rep"), scatter_dimension=1, tiled=True),
        lax.psum_scatter(grads[20], ("fsdp", "rep"), scatter_dimension=1, tiled=True),
        lax.psum_scatter(grads[21], ("fsdp", "rep"), scatter_dimension=0, tiled=True),
    )
    totals = lax.psum(
        (grads[7], grads[8], grads[13], grads[14], grads[22], grads[23], grads[24]), ("fsdp", "rep")
    )
    return (
        rgb,
        anchors_grad,
        directions_grad,
        deltas_grad,
        shares[0],
        shares[1],
        shares[2],
        shares[3],
        shares[4],
        shares[5],
        shares[6],
        totals[0],
        totals[1],
        shares[7],
        shares[8],
        shares[9],
        shares[10],
        totals[2],
        totals[3],
        shares[11],
        shares[12],
        shares[13],
        shares[14],
        shares[15],
        shares[16],
        shares[17],
        totals[4],
        totals[5],
        totals[6],
    )


def solution(mesh):
    placed = (
        P(None, ("fsdp", "rep")),
        P(None, ("fsdp", "rep")),
        P(("fsdp", "rep"), None),
        P(("fsdp", "rep"), None),
        P(None, ("fsdp", "rep")),
        P(("fsdp", "rep")),
        P(("fsdp", "rep")),
        P(None, None, ("fsdp", "rep")),
        P(None, ("fsdp", "rep")),
        P(None, ("fsdp", "rep")),
        P(("fsdp", "rep"), None),
        P(),
        P(),
        P(None, ("fsdp", "rep")),
        P(("fsdp", "rep")),
        P(("fsdp", "rep")),
        P(("fsdp", "rep"), None),
        P(),
        P(),
        P(None, ("fsdp", "rep")),
        P(("fsdp", "rep")),
        P(("fsdp", "rep")),
        P(None, None, ("fsdp", "rep")),
        P(None, ("fsdp", "rep")),
        P(None, ("fsdp", "rep")),
        P(("fsdp", "rep"), None),
        P(),
        P(),
        P(),
        P(None, ("fsdp", "rep")),
    )
    return jax.shard_map(
        per_device,
        mesh=mesh,
        in_specs=placed,
        out_specs=(
            P(None, ("fsdp", "rep")),
            P(None, ("fsdp", "rep")),
            P(None, ("fsdp", "rep")),
            P(("fsdp", "rep"), None),
            P(None, ("fsdp", "rep")),
            P(("fsdp", "rep")),
            P(("fsdp", "rep")),
            P(None, None, ("fsdp", "rep")),
            P(None, ("fsdp", "rep")),
            P(None, ("fsdp", "rep")),
            P(("fsdp", "rep"), None),
            P(),
            P(),
            P(None, ("fsdp", "rep")),
            P(("fsdp", "rep")),
            P(("fsdp", "rep")),
            P(("fsdp", "rep"), None),
            P(),
            P(),
            P(None, ("fsdp", "rep")),
            P(("fsdp", "rep")),
            P(("fsdp", "rep")),
            P(None, None, ("fsdp", "rep")),
            P(None, ("fsdp", "rep")),
            P(None, ("fsdp", "rep")),
            P(("fsdp", "rep"), None),
            P(),
            P(),
            P(),
        ),
        check_vma=False,
    )
```

profile of v0, /device:TPU:0, one launch (start us, length us, event | category | flops | bytes accessed | tf_op | source)
XLA Modules:
  0.0 1273.0 jit_solution(579907480654974308)
XLA Ops:
  12.4 42.1 %all-reduce.96 = (bf16[256]{0:T(256)(128)(2,1)S(1)}, bf16[256]{0:T(256)(128)(2,1)S(1)}, bf16[256]{0:T(256)(128)(2,1)S(1)}, bf16[256]{0:T(256)(128)(2,1)S(1)}, bf...) all-reduce(bf16[256]{0:T(256)(128)(2,1)S(1)} %dynamic-update-slice., ...), channel_id=1, replica_groups=mesh['fsdp'=8,'rep'=4] {'fsdp','rep'}, use_global_device_ids=true, to_apply=%add.75 | all-reduce | flops 1536 | bytes 6144
  58.3 40.5 %all-gather = bf16[32,8,4]{1,2,0:T(4,128)(2,1)S(1)} all-gather(bf16[1,8,4]{1,2,0:T(4,128)(2,1)} %bitcast.521), channel_id=1, replica_groups=mesh['fsdp'=8,'rep'=4] {'fsdp','rep'}, dimensions={0}, use_global_device_ids=true | all-gather | bytes 2112 | tf_op jit(solution)/shard_map/all_gather | solution.py:193
  99.0 36.9 %all-gather.1 = bf16[32,8,4]{1,2,0:T(4,128)(2,1)S(1)} all-gather(bf16[1,8,4]{1,2,0:T(4,128)(2,1)} %bitcast.522), channel_id=1, replica_groups=mesh['fsdp'=8,'rep'=4] {'fsdp','rep'}, dimensions={0}, use_global_device_ids=true | all-gather | bytes 2112 | tf_op jit(solution)/shard_map/all_gather | solution.py:194
  137.8 38.4 %all_gather.72 = bf16[39,256]{0,1:T(8,128)(2,1)S(1)} all-gather(bf16[39,8]{0,1:T(8,128)(2,1)} %param.37), channel_id=1, replica_groups=mesh['fsdp'=8,'rep'=4] {'fsdp','rep'}, dimensions={1}, use_global_device_ids=true | all-gather | bytes 20592 | tf_op jit(solution)/shard_map/all_gather | solution.py:189
  176.4 37.2 %all_gather.78 = bf16[256,217]{1,0:T(8,128)(2,1)S(1)} all-gather(bf16[8,217]{1,0:T(8,128)(2,1)} %param.43), channel_id=1, replica_groups=mesh['fsdp'=8,'rep'=4] {'fsdp','rep'}, dimensions={0}, use_global_device_ids=true | all-gather | bytes 114576 | tf_op jit(solution)/shard_map/all_gather | solution.py:195
  213.8 38.5 %all_gather.79 = bf16[256,256]{0,1:T(8,128)(2,1)S(1)} all-gather(bf16[256,8]{0,1:T(8,128)(2,1)} %param.46), channel_id=1, replica_groups=mesh['fsdp'=8,'rep'=4] {'fsdp','rep'}, dimensions={1}, use_global_device_ids=true | all-gather | bytes 135168 | tf_op jit(solution)/shard_map/all_gather | solution.py:196
  252.6 37.4 %all_gather.82 = bf16[256,257]{1,0:T(8,128)(2,1)S(1)} all-gather(bf16[8,257]{1,0:T(8,128)(2,1)} %param.49), channel_id=1, replica_groups=mesh['fsdp'=8,'rep'=4] {'fsdp','rep'}, dimensions={0}, use_global_device_ids=true | all-gather | bytes 135696 | tf_op jit(solution)/shard_map/all_gather | solution.py:199
  290.3 39.5 %all_gather.75 = bf16[4,256,256]{1,0,2:T(4,128)(2,1)S(1)} all-gather(bf16[4,256,8]{1,0,2:T(4,128)(2,1)S(1)} %copy.147), channel_id=1, replica_groups=mesh['fsdp'=8,'rep'=4] {'fsdp','rep'}, dimensions={2}, use_global_device_ids=true | all-gather | bytes 540672 | tf_op jit(solution)/shard_map/all_gather | solution.py:192
  331.6 3.1 multiply_sine_fusion
  344.2 6.9 fusion.106
  351.1 21.6 %concatenate.60 = f32[4096,256]{0,1:T(8,128)} concatenate(f32[4096,217]{0,1:T(8,128)} %get-tuple-element.502, f32[4096,3]{0,1:T(4,128)S(1)} %get-tuple-element.369, f32[4096,3]{0,1:T(4,128)S(1)} %get-tuple-element.424, f32[4096,3]{0,1:T(4,128)S(1)} %get-tuple-element.423, f32[4096,3]{0,1:T(4,128)S(1)} %get-tuple-element.422, f32[4096,3]{0,1:T(4,128)S(1)} %get-tuple-element.414, ...), dimensions={1} | concatenate | bytes 8388608 | tf_op jit(solution)/shard_map/jvp()/concatenate | solution.py:53
  372.7 3.0 fusion.2
  381.1 2.8 convolution_add_fusion
  388.1 4.2 fusion.57
  392.3 4.0 fusion.55
  396.4 4.0 fusion.53
  400.4 3.6 fusion.51
  405.9 4.0 fusion.49
  410.0 4.2 fusion.47
  414.4 4.7 fusion.63
  420.0 5.3 fusion.181
  430.4 36.7 %all-gather.2 = bf16[32,8,3]{1,2,0:T(4,128)(2,1)S(1)} all-gather(bf16[1,8,3]{1,2,0:T(4,128)(2,1)S(1)} %bitcast.523), channel_id=1, replica_groups=mesh['fsdp'=8,'rep'=4] {'fsdp','rep'}, dimensions={0}, use_global_device_ids=true | all-gather | bytes 1584 | tf_op jit(solution)/shard_map/all_gather | solution.py:204
  467.2 38.0 %all-gather.3 = bf16[32,8,3]{1,2,0:T(4,128)(2,1)S(1)} all-gather(bf16[1,8,3]{1,2,0:T(4,128)(2,1)S(1)} %bitcast.524), channel_id=1, replica_groups=mesh['fsdp'=8,'rep'=4] {'fsdp','rep'}, dimensions={0}, use_global_device_ids=true | all-gather | bytes 1584 | tf_op jit(solution)/shard_map/all_gather | solution.py:205
  505.3 36.7 %all-gather.4 = bf16[32,8,3]{1,2,0:T(4,128)(2,1)S(1)} all-gather(bf16[1,8,3]{1,2,0:T(4,128)(2,1)S(1)} %bitcast.525), channel_id=1, replica_groups=mesh['fsdp'=8,'rep'=4] {'fsdp','rep'}, dimensions={0}, use_global_device_ids=true | all-gather | bytes 1584 | tf_op jit(solution)/shard_map/all_gather | solution.py:206
  544.1 38.5 %all_gather.83 = bf16[289,256]{0,1:T(8,128)(2,1)S(1)} all-gather(bf16[289,8]{0,1:T(8,128)(2,1)S(1)} %copy-done.203), channel_id=1, replica_groups=mesh['fsdp'=8,'rep'=4] {'fsdp','rep'}, dimensions={1}, use_global_device_ids=true | all-gather | bytes 152592 | tf_op jit(solution)/shard_map/all_gather | solution.py:200
  582.8 37.7 %all_gather.86 = bf16[3,256,256]{1,2,0:T(8,128)(2,1)S(1)} all-gather(bf16[3,256,8]{1,2,0:T(8,128)(2,1)S(1)} %copy-done.162), channel_id=1, replica_groups=mesh['fsdp'=8,'rep'=4] {'fsdp','rep'}, dimensions={2}, use_global_device_ids=true | all-gather | bytes 405504 | tf_op jit(solution)/shard_map/all_gather | solution.py:203
  627.1 16.7 %concatenate.62 = bf16[4096,289]{0,1:T(8,128)(2,1)S(1)} concatenate(bf16[4096,3]{0,1:T(4,128)(2,1)} %copy-done.63, bf16[4096,3]{0,1:T(4,128)(2,1)} %bitcast.458, bf16[4096,3]{0,1:T(4,128)(2,1)} %get-tuple-element.437, bf16[4096,3]{0,1:T(4,128)(2,1)} %get-tuple-element.436, bf16[4096,3]{0,1:T(4,128)(2,1)} %get-tuple-element.435, bf16[4096,3]{0,1:T(4,128)(2,1)} %get-tuple-element.432, ...), dimensions={1} | concatenate | bytes 4734976 | tf_op jit(solution)/shard_map/concatenate | solution.py:66
  650.0 3.5 multiply_convert_fusion.7
  661.1 4.8 fusion.455
  680.7 3.0 fusion.7
  689.5 4.9 split.324
  695.8 4.8 fusion.409
  704.0 7.2 multiply_convert_fusion.6
  711.2 4.5 fusion.123
  715.6 5.2 multiply_convert_fusion.5
  720.8 4.5 fusion.124
  725.3 5.2 multiply_convert_fusion.4
  730.5 5.9 multiply_multiply_fusion.6
  736.4 21.2 %concatenate.73 = f32[4096,256]{0,1:T(8,128)} concatenate(f32[4096,217]{0,1:T(8,128)} %get-tuple-element.513, f32[4096,3]{0,1:T(4,128)S(1)} %get-tuple-element.327, f32[4096,3]{0,1:T(4,128)S(1)} %get-tuple-element.402, f32[4096,3]{0,1:T(4,128)S(1)} %get-tuple-element.400, f32[4096,3]{0,1:T(4,128)S(1)} %get-tuple-element.395, f32[4096,3]{0,1:T(4,128)S(1)} %get-tuple-element.397, ...), dimensions={1} | concatenate | bytes 8388608 | tf_op jit(solution)/shard_map/transpose(jvp(transpose(jvp())))/concatenate | solution.py:53
  757.7 8.9 multiply_convert_fusion.2
  766.5 4.5 fusion.126
  771.0 5.3 multiply_convert_fusion.1
  776.3 4.5 fusion.127
  780.8 2.8 convolution_multiply_fusion
  788.4 6.4 fusion.122
  795.6 8.2 fusion.450
  803.8 4.4 fusion.158
  809.3 5.7 fusion.449
  815.0 5.8 fusion.451
  828.7 5.4 fusion.406
  834.1 8.7 fusion.448
  842.8 5.8 fusion.447
  854.3 2.8 multiply_reduce_fusion.6
  863.0 5.6 convolution_convert_fusion.30
  869.1 3.3 fusion.171
  874.0 8.8 fusion.125
  885.8 6.0 fusion.446
  892.3 4.2 fusion.277
  900.3 3.4 fusion.107
  909.8 3.9 fusion.182
  920.7 39.9 %all-reduce.101 = (f32[39,256]{1,0:T(8,128)S(1)}, f32[256]{0:T(256)S(1)}, f32[256]{0:T(256)S(1)}, f32[4,256]{1,0:T(4,128)S(1)}, f32[4,256]{1,0:T(4,128)S(1)}, /*...) all-reduce(f32[39,256]{1,0:T(8,128)S(1)} %add_add_fusion.11, ...), channel_id=2, replica_groups=mesh['fsdp'=8,'rep'=4] {'fsdp','rep'}, use_global_device_ids=true, to_apply=%region_25.29.clone | all-reduce | flops 16827 | bytes 134616
  974.6 23.5 %all-reduce.100.cloned.1.call-done = (f32[4,256,256]{1,0,2:T(4,128)}, f32[256,257]{0,1:T(8,128)}, f32[289,256]{1,0:T(8,128)}, f32[3,256,256]{1,0,2:T(4,128)}) async-done(((f32[4,256,256]{1,0,2:T(4,128)}, f32[256,257]{0,1:T(8,128)}, f32[289,256]{1,0:T(8,128)}, f32[3,256,256]{1,0,2:T(4,128)}), (f32[4,256,256]{1,0,2:T(4,128)}, f32[256,257]{0,1:T(8,128)}, f32[289,256]{1,0:T(8,128)}, ...) | async-done | bytes 2394128
  1004.3 129.5 %reduce-scatter.15.cloned.1.call-done = f32[8,217]{1,0:T(8,128)} async-done(((f32[256,217]{1,0:T(8,128)}), f32[8,217]{1,0:T(8,128)}) %reduce-scatter.15.cloned.1.call-update) | async-done | bytes 6960
  1133.9 132.2 %reduce-scatter.17.cloned.1.call-done = f32[8,256]{1,0:T(8,128)} async-done(((f32[256,256]{1,0:T(8,128)}), f32[8,256]{1,0:T(8,128)}) %reduce-scatter.17.cloned.1.call-update) | async-done | bytes 8208
  (909 shorter events, 152.3 us)
Async XLA Ops:
  7.2 128.7 %copy-start = (f32[3,32]{1,0:T(4,128)S(1)}, f32[3,32]{1,0:T(4,128)}, u32[]{:S(2)}) copy-start(f32[3,32]{1,0:T(4,128)} %param.34) | copy-start | bytes 1156
  7.2 990.9 %all-reduce.100.cloned.1.call-start = ((), (), s32[]{:S(2)}) async-start(), calls=%async_computation.4 | async-start | bytes 5341184
  54.5 280.3 %copy-start.234 = (bf16[256]{0:T(256)(128)(2,1)}, bf16[256]{0:T(256)(128)(2,1)S(1)}, u32[]{:S(2)}) copy-start(bf16[256]{0:T(256)(128)(2,1)S(1)} %get-tuple-element.313) | copy-start | bytes 1540
  54.5 280.9 %copy-start.236 = (bf16[256]{0:T(256)(128)(2,1)}, bf16[256]{0:T(256)(128)(2,1)S(1)}, u32[]{:S(2)}) copy-start(bf16[256]{0:T(256)(128)(2,1)S(1)} %get-tuple-element.314) | copy-start | bytes 1540
  57.6 277.8 %copy-start.232 = (bf16[217]{0:T(256)(128)(2,1)S(1)}, bf16[217]{0:T(256)(128)(2,1)}, u32[]{:S(2)}) copy-start(bf16[217]{0:T(256)(128)(2,1)} %param.44) | copy-start | bytes 1306
  57.6 277.8 %copy-start.215 = (bf16[257]{0:T(512)(128)(2,1)S(1)}, bf16[257]{0:T(512)(128)(2,1)}, u32[]{:S(2)}) copy-start(bf16[257]{0:T(512)(128)(2,1)} %param.50) | copy-start | bytes 1546
  58.3 273.3 %copy-start.133 = (f32[32,128]{1,0:T(8,128)}, f32[32,128]{1,0:T(8,128)S(1)}, u32[]{:S(2)}) copy-start(f32[32,128]{1,0:T(8,128)S(1)} %multiply_subtract_fusion) | copy-start | bytes 49156
  136.0 559.8 %copy-start.40 = (f32[1,3,32,128]{3,2,1,0:T(8,128)}, f32[1,3,32,128]{3,2,1,0:T(8,128)S(1)}, u32[]{:S(2)}) copy-start(f32[1,3,32,128]{3,2,1,0:T(8,128)S(1)} %broadcast_bitcast_fusion.1) | copy-start | bytes 147460
  176.3 237.9 %copy-start.52 = (bf16[39,256]{1,0:T(8,128)(2,1)}, bf16[39,256]{1,0:T(8,128)(2,1)S(1)}, u32[]{:S(2)}) copy-start(bf16[39,256]{1,0:T(8,128)(2,1)S(1)} %copy.146) | copy-start | bytes 59908
  176.3 161.4 %copy-start.191 = (f32[256]{0:T(256)}, f32[256]{0:T(256)S(1)}, u32[]{:S(2)}) copy-start(f32[256]{0:T(256)S(1)} %fusion.275) | copy-start | bytes 3076
  213.7 186.7 %copy-start.44 = (bf16[256,217]{0,1:T(8,128)(2,1)}, bf16[256,217]{0,1:T(8,128)(2,1)S(1)}, u32[]{:S(2)}) copy-start(bf16[256,217]{0,1:T(8,128)(2,1)S(1)} %copy.153) | copy-start | bytes 333316
  213.8 124.0 %copy-start.173 = (f32[217]{0:T(256)}, f32[217]{0:T(256)S(1)}, u32[]{:S(2)}) copy-start(f32[217]{0:T(256)S(1)} %fusion.169) | copy-start | bytes 2608
  252.5 143.8 %copy-start.12 = (bf16[256,256]{1,0:T(8,128)(2,1)}, bf16[256,256]{1,0:T(8,128)(2,1)S(1)}, u32[]{:S(2)}) copy-start(bf16[256,256]{1,0:T(8,128)(2,1)S(1)} %copy.154) | copy-start | bytes 393220
  252.6 85.2 %copy-start.171 = (f32[256]{0:T(256)}, f32[256]{0:T(256)S(1)}, u32[]{:S(2)}) copy-start(f32[256]{0:T(256)S(1)} %fusion.166) | copy-start | bytes 3076
  290.1 96.4 %copy-start.41 = (bf16[256,257]{0,1:T(8,128)(2,1)}, bf16[256,257]{0,1:T(8,128)(2,1)S(1)}, u32[]{:S(2)}) copy-start(bf16[256,257]{0,1:T(8,128)(2,1)S(1)} %copy.155) | copy-start | bytes 394756
  290.3 47.5 %copy-start.155 = (f32[257]{0:T(512)}, f32[257]{0:T(512)S(1)}, u32[]{:S(2)}) copy-start(f32[257]{0:T(512)S(1)} %fusion.156) | copy-start | bytes 3088
  331.6 368.9 %copy-start.27 = (f32[4096,3]{0,1:T(4,128)}, f32[4096,3]{0,1:T(4,128)S(1)}, u32[]{:S(2)}) copy-start(f32[4096,3]{0,1:T(4,128)S(1)} %get-tuple-element.369) | copy-start | bytes 147460
  334.7 84.4 %copy-start.36 = (f32[4096,3]{0,1:T(4,128)}, f32[4096,3]{0,1:T(4,128)S(1)}, u32[]{:S(2)}) copy-start(f32[4096,3]{0,1:T(4,128)S(1)} %get-tuple-element.424) | copy-start | bytes 147460
  334.7 365.9 %copy-start.34 = (f32[4096,3]{0,1:T(4,128)}, f32[4096,3]{0,1:T(4,128)S(1)}, u32[]{:S(2)}) copy-start(f32[4096,3]{0,1:T(4,128)S(1)} %get-tuple-element.423) | copy-start | bytes 147460
  335.4 65.0 %copy-start.212 = (f32[217]{0:T(256)}, f32[217]{0:T(256)S(1)}, u32[]{:S(2)}) copy-start(f32[217]{0:T(256)S(1)} %convert_multiply_fusion.34) | copy-start | bytes 2608
  335.4 60.9 %copy-start.157 = (f32[256]{0:T(256)}, f32[256]{0:T(256)S(1)}, u32[]{:S(2)}) copy-start(f32[256]{0:T(256)S(1)} %convert_multiply_fusion.32) | copy-start | bytes 3076
  335.4 51.1 %copy-start.201 = (f32[257]{0:T(512)}, f32[257]{0:T(512)S(1)}, u32[]{:S(2)}) copy-start(f32[257]{0:T(512)S(1)} %rsqrt_multiply_fusion.1) | copy-start | bytes 3088
  338.6 49.4 %copy-start.50 = (bf16[256,256]{1,0:T(8,128)(2,1)}, bf16[256,256]{1,0:T(8,128)(2,1)S(1)}, u32[]{:S(2)}) copy-start(bf16[256,256]{1,0:T(8,128)(2,1)S(1)} %get-tuple-element.375) | copy-start | bytes 393220
  338.7 53.6 %copy-start.140 = (bf16[256,256]{1,0:T(8,128)(2,1)}, bf16[256,256]{1,0:T(8,128)(2,1)S(1)}, u32[]{:S(2)}) copy-start(bf16[256,256]{1,0:T(8,128)(2,1)S(1)} %get-tuple-element.378) | copy-start | bytes 393220
  338.7 65.3 %copy-start.137 = (bf16[256,256]{1,0:T(8,128)(2,1)}, bf16[256,256]{1,0:T(8,128)(2,1)S(1)}, u32[]{:S(2)}) copy-start(bf16[256,256]{1,0:T(8,128)(2,1)S(1)} %get-tuple-element.376) | copy-start | bytes 393220
  338.7 71.3 %copy-start.134 = (bf16[256,256]{1,0:T(8,128)(2,1)}, bf16[256,256]{1,0:T(8,128)(2,1)S(1)}, u32[]{:S(2)}) copy-start(bf16[256,256]{1,0:T(8,128)(2,1)S(1)} %get-tuple-element.377) | copy-start | bytes 393220
  375.6 20.7 %copy-start.7 = (f32[4096,256]{1,0:T(8,128)}, f32[4096,256]{1,0:T(8,128)S(1)}, u32[]{:S(2)}) copy-start(f32[4096,256]{1,0:T(8,128)S(1)} %fusion.2) | copy-start | bytes 12582916
  384.0 41.4 %copy-start.64 = (f32[4096,1]{0,1:T(1,128)}, f32[4096,1]{0,1:T(1,128)S(1)}, u32[]{:S(2)}) copy-start(f32[4096,1]{0,1:T(1,128)S(1)} %slice.392) | copy-start | bytes 49156
  414.3 52.9 %copy-start.243 = (bf16[3,8]{1,0:T(4,128)(2,1)S(1)}, bf16[3,8]{1,0:T(4,128)(2,1)}, u32[]{:S(2)}) copy-start(bf16[3,8]{1,0:T(4,128)(2,1)} %param.57) | copy-start | bytes 148
  414.3 91.0 %copy-start.244 = (bf16[8,3]{0,1:T(4,128)(2,1)S(1)}, bf16[8,3]{0,1:T(4,128)(2,1)}, u32[]{:S(2)}) copy-start(bf16[8,3]{0,1:T(4,128)(2,1)} %param.58) | copy-start | bytes 148
  414.3 129.0 %copy-start.231 = (f32[3,32]{1,0:T(4,128)S(1)}, f32[3,32]{1,0:T(4,128)}, u32[]{:S(2)}) copy-start(f32[3,32]{1,0:T(4,128)} %param.62) | copy-start | bytes 1156
  414.3 129.7 %copy-start.203 = (bf16[289,8]{0,1:T(8,128)(2,1)S(1)}, bf16[289,8]{0,1:T(8,128)(2,1)}, u32[]{:S(2)}) copy-start(bf16[289,8]{0,1:T(8,128)(2,1)} %param.52) | copy-start | bytes 13876
  414.3 168.4 %copy-start.162 = (bf16[3,256,8]{1,2,0:T(8,128)(2,1)S(1)}, bf16[3,256,8]{1,2,0:T(8,128)(2,1)}, u32[]{:S(2)}) copy-start(bf16[3,256,8]{1,2,0:T(8,128)(2,1)} %param.55) | copy-start | bytes 36868
  420.0 205.6 %copy-start.250 = (bf16[3]{0:T(256)(128)(2,1)S(1)}, bf16[3]{0:T(256)(128)(2,1)}, u32[]{:S(2)}) copy-start(bf16[3]{0:T(256)(128)(2,1)} %param.59) | copy-start | bytes 22
  420.0 206.1 %copy-start.240 = (bf16[256]{0:T(256)(128)(2,1)S(1)}, bf16[256]{0:T(256)(128)(2,1)}, u32[]{:S(2)}) copy-start(bf16[256]{0:T(256)(128)(2,1)} %get-tuple-element.316) | copy-start | bytes 1540
  425.4 201.5 %copy-start.46 = (f32[4096,3]{0,1:T(4,128)}, f32[4096,3]{0,1:T(4,128)S(1)}, u32[]{:S(2)}) copy-start(f32[4096,3]{0,1:T(4,128)S(1)} %get-tuple-element.367) | copy-start | bytes 147460
  425.4 201.5 %copy-start.55 = (f32[4096]{0:T(1024)}, f32[4096]{0:T(1024)S(1)}, u32[]{:S(2)}) copy-start(f32[4096]{0:T(1024)S(1)} %get-tuple-element.366) | copy-start | bytes 49156
  426.1 200.8 %copy-start.117 = (f32[32,128]{1,0:T(8,128)}, f32[32,128]{1,0:T(8,128)S(1)}, u32[]{:S(2)}) copy-start(f32[32,128]{1,0:T(8,128)S(1)} %get-tuple-element.361) | copy-start | bytes 49156
  426.5 200.4 %copy-start.131 = (f32[32,63]{1,0:T(8,128)}, f32[32,63]{1,0:T(8,128)S(1)}, u32[]{:S(2)}) copy-start(f32[32,63]{1,0:T(8,128)S(1)} %slice.365) | copy-start | bytes 24196
  427.4 199.5 %copy-start.129 = (f32[32,31]{1,0:T(8,128)}, f32[32,31]{1,0:T(8,128)S(1)}, u32[]{:S(2)}) copy-start(f32[32,31]{1,0:T(8,128)S(1)} %slice.363) | copy-start | bytes 11908
  428.0 198.9 %copy-start.127 = (f32[32,15]{1,0:T(8,128)}, f32[32,15]{1,0:T(8,128)S(1)}, u32[]{:S(2)}) copy-start(f32[32,15]{1,0:T(8,128)S(1)} %slice.361) | copy-start | bytes 5764
  428.4 198.5 %copy-start.125 = (f32[32,7]{1,0:T(8,128)}, f32[32,7]{1,0:T(8,128)S(1)}, u32[]{:S(2)}) copy-start(f32[32,7]{1,0:T(8,128)S(1)} %slice.359) | copy-start | bytes 2692
  428.6 113.3 %copy-start.111 = (f32[32,8]{1,0:T(8,128)}, f32[32,8]{1,0:T(8,128)S(1)}, u32[]{:S(2)}) copy-start(f32[32,8]{1,0:T(8,128)S(1)} %slice.344) | copy-start | bytes 3076
  428.7 198.2 %copy-start.123 = (f32[32,3]{1,0:T(8,128)}, f32[32,3]{1,0:T(8,128)S(1)}, u32[]{:S(2)}) copy-start(f32[32,3]{1,0:T(8,128)S(1)} %slice.357) | copy-start | bytes 1156
  428.8 113.1 %copy-start.113 = (f32[32,4]{1,0:T(8,128)}, f32[32,4]{1,0:T(8,128)S(1)}, u32[]{:S(2)}) copy-start(f32[32,4]{1,0:T(8,128)S(1)} %slice.348) | copy-start | bytes 1540
  428.9 113.0 %copy-start.115 = (f32[32,4]{1,0:T(8,128)}, f32[32,4]{1,0:T(8,128)S(1)}, u32[]{:S(2)}) copy-start(f32[32,4]{1,0:T(8,128)S(1)} %slice.347) | copy-start | bytes 1540
  428.9 114.4 %copy-start.48 = (f32[32,4]{1,0:T(8,128)}, f32[32,4]{1,0:T(8,128)S(1)}, u32[]{:S(2)}) copy-start(f32[32,4]{1,0:T(8,128)S(1)} %mul.2031) | copy-start | bytes 1540
  429.0 114.3 %copy-start.119 = (f32[32,2]{1,0:T(8,128)}, f32[32,2]{1,0:T(8,128)S(1)}, u32[]{:S(2)}) copy-start(f32[32,2]{1,0:T(8,128)S(1)} %slice.351) | copy-start | bytes 772
  429.1 114.2 %copy-start.121 = (f32[32,2]{1,0:T(8,128)}, f32[32,2]{1,0:T(8,128)S(1)}, u32[]{:S(2)}) copy-start(f32[32,2]{1,0:T(8,128)S(1)} %slice.350) | copy-start | bytes 772
  429.1 114.2 %copy-start.59 = (f32[32,2]{1,0:T(8,128)}, f32[32,2]{1,0:T(8,128)S(1)}, u32[]{:S(2)}) copy-start(f32[32,2]{1,0:T(8,128)S(1)} %mul.2032) | copy-start | bytes 772
  429.2 114.1 %copy-start.86 = (f32[32,1]{1,0:T(8,128)}, f32[32,1]{1,0:T(8,128)S(1)}, u32[]{:S(2)}) copy-start(f32[32,1]{1,0:T(8,128)S(1)} %get-tuple-element.467) | copy-start | bytes 388
  429.2 114.2 %copy-start.88 = (f32[32,1]{1,0:T(8,128)}, f32[32,1]{1,0:T(8,128)S(1)}, u32[]{:S(2)}) copy-start(f32[32,1]{1,0:T(8,128)S(1)} %get-tuple-element.468) | copy-start | bytes 388
  542.2 118.9 %copy-start.144 = (f32[256,3]{0,1:T(4,128)}, f32[256,3]{0,1:T(4,128)S(1)}, u32[]{:S(2)}) copy-start(f32[256,3]{0,1:T(4,128)S(1)} %reshape.432) | copy-start | bytes 9220
  542.4 84.6 %copy-start.238 = (f32[3]{0:T(128)}, f32[3]{0:T(128)S(1)}, u32[]{:S(2)}) copy-start(f32[3]{0:T(128)S(1)} %multiply_reduce_fusion.17) | copy-start | bytes 40
  582.7 97.6 %copy-start.20 = (bf16[289,256]{1,0:T(8,128)(2,1)}, bf16[289,256]{1,0:T(8,128)(2,1)S(1)}, u32[]{:S(2)}) copy-start(bf16[289,256]{1,0:T(8,128)(2,1)S(1)} %copy.156) | copy-start | bytes 443908
  582.8 44.2 %copy-start.177 = (f32[256]{0:T(256)}, f32[256]{0:T(256)S(1)}, u32[]{:S(2)}) copy-start(f32[256]{0:T(256)S(1)} %fusion.153) | copy-start | bytes 3076
  626.2 54.1 %copy-start.159 = (f32[256]{0:T(256)}, f32[256]{0:T(256)S(1)}, u32[]{:S(2)}) copy-start(f32[256]{0:T(256)S(1)} %convert_multiply_fusion.30) | copy-start | bytes 3076
  700.6 35.8 %copy-start.43 = (f32[4096,3]{0,1:T(4,128)}, f32[4096,3]{0,1:T(4,128)S(1)}, u32[]{:S(2)}) copy-start(f32[4096,3]{0,1:T(4,128)S(1)} %get-tuple-element.327) | copy-start | bytes 147460
  736.4 21.2 %copy-start.13 = (bf16[256,256]{1,0:T(8,128)(2,1)S(1)}, bf16[256,256]{1,0:T(8,128)(2,1)}, u32[]{:S(2)}) copy-start(bf16[256,256]{1,0:T(8,128)(2,1)} %copy-done.12) | copy-start | bytes 393220
  736.4 21.2 %copy-start.158 = (f32[256]{0:T(256)S(1)}, f32[256]{0:T(256)}, u32[]{:S(2)}) copy-start(f32[256]{0:T(256)} %copy-done.157) | copy-start | bytes 3076
  862.7 271.2 %reduce-scatter.15.cloned.1.call-start = ((), (), s32[]{:S(2)}) async-start(), calls=%async_computation.2 | async-start | bytes 270336
  874.0 392.1 %reduce-scatter.17.cloned.1.call-start = ((), (), s32[]{:S(2)}) async-start(), calls=%async_computation.3 | async-start | bytes 270336
  900.2 16.9 %copy-start.184 = (f32[256]{0:T(256)S(1)}, f32[256]{0:T(256)}, u32[]{:S(2)}) copy-start(f32[256]{0:T(256)} %copy-done.183) | copy-start | bytes 3076
  900.2 365.8 %copy-start.1 = (f32[3,32]{1,0:T(4,128)S(1)}, f32[3,32]{1,0:T(4,128)}, u32[]{:S(2)}) copy-start(f32[3,32]{1,0:T(4,128)} %param.34) | copy-start | bytes 1156
  (246 other events, 1180.7 us)
Sparse Core Ops, SparseCore 0:
  862.8 135.2 all-reduce.99
  1001.0 132.7 reduce-scatter.14
  1136.7 129.3 reduce-scatter.16
where the time goes:
time: 1280 us; the launch traced here: 1270 us
  blocking collectives  538 us (42%)
  waiting for transfers between devices  285 us (22%)
  matrix products  236 us (18%)
  local copies, waits for them, and re-layouts  126 us (10%)
  other arithmetic  66.8 us (5%)
  between operations  20.6 us (2%)
    unnamed x6, waiting for transfers between devices  285 us
    dot_general x62, matrix products, project(): jnp.dot(rows.astype(jnp.bfloat16), weight.astype(jnp.bfloat16), preferred...  236 us
    unnamed x2, blocking collectives  82 us
    concatenate x2, local copies, waits for them, and re-layouts, sdf_net(): hidden = jnp.concatenate([hidden, encoded], axis=1) * root_half  42.8 us
    unnamed x655, local copies, waits for them, and re-layouts  41.3 us
    all_gather x1, blocking collectives, per_device(): lax.all_gather(sdf_mid_gain, ('fsdp', 'rep'), axis=1, tiled=True)  40.5 us
    all_gather x1, blocking collectives, per_device(): lax.all_gather(sdf_mid_dir, ('fsdp', 'rep'), axis=2, tiled=True)  39.5 us
    all_gather x1, blocking collectives, per_device(): lax.all_gather(sdf_skip_dir, ('fsdp', 'rep'), axis=1, tiled=True)  38.5 us
  transfers between devices with their start and end apart: 3, of which 3 were waited for; matrix products, arithmetic and copies ran while one was open for 6% of the time, Pallas kernels for 0%

commit v1 on v0

v1 whole, which is shorter than its diff:
```python
import functools

import jax
import jax.numpy as jnp
from jax import lax
from jax.experimental import pallas as pl
from jax.experimental.pallas import tpu as pltpu
from jax.sharding import PartitionSpec as P

F32 = jnp.float32
BF = jnp.bfloat16
H = 256
SAMP = 128
ENC = 39
EROWS = 48
NARROW = 217
NX = 33
GROUPS = 12
SUB = 256
RC = 8
PTS = RC * SAMP
NSUB = PTS // SUB
RSUB = SUB // SAMP
CROSS = 128
BIASES = 200
TAIL = 216
EPS = 1e-06
HALF_LN2 = 0.34657359027997264
ROOT_HALF = 0.7071067811865476


def nn(a, b):
    return lax.dot_general(a, b, (((1,), (0,)), ((), ())), preferred_element_type=F32)


def nt(a, b):
    return lax.dot_general(a, b, (((1,), (1,)), ((), ())), preferred_element_type=F32)


def exact(a, b):
    return lax.dot_general(
        a, b, (((1,), (0,)), ((), ())), precision=lax.Precision.HIGHEST, preferred_element_type=F32
    )


def iota(shape, dim):
    return lax.broadcasted_iota(jnp.int32, shape, dim)


def column(row):
    n = row.shape[1]
    return jnp.sum(jnp.where(iota((n, n), 0) == iota((n, n), 1), row, 0.0), axis=1, keepdims=True)


def as_row(ref):
    return ref[...].astype(F32).reshape(1, ref.shape[0])


def line(col):
    n = col.shape[0]
    return jnp.sum(jnp.where(iota((n, n), 0) == iota((n, n), 1), col, 0.0), axis=0, keepdims=True)


def wide(half):
    return jnp.concatenate([half, half], axis=1)


def sharp(z):
    z = z.astype(BF)
    s = 0.5 * jnp.tanh(z) + 0.5
    return jnp.maximum(z, 0.0) - 0.5 * jnp.log(jnp.maximum(s, 1.0 - s)), s


def silu(z):
    z = z.astype(BF)
    g = 0.5 * jnp.tanh(0.5 * z) + 0.5
    h = z * g
    return h, g + h * (1.0 - g)


def softplus(x):
    return jnp.maximum(x, 0.0) + jnp.log(1.0 + jnp.exp(-jnp.abs(x)))


def sigmoid(x):
    return 1.0 / (1.0 + jnp.exp(-x))


def scaled_rows(d, gain):
    return d * (gain * lax.rsqrt(jnp.sum(d * d, axis=1, keepdims=True) + EPS))


def share_rows(first, narrow, last, cfirst, wid):
    r = first.shape[0]

    def padded(k, ref, lanes):
        wid[k] = jnp.zeros(wid.shape[1:], F32)
        wid[k, :, 0 : ref.shape[1]] = ref[...].astype(F32)
        return wid[k][:, 0:lanes]

    return (padded(0, first, 128), padded(1, narrow, H), padded(2, last, 384), padded(3, cfirst, 384))


class Place:
    def __init__(self, fsdp):
        f, p = lax.axis_index("fsdp"), lax.axis_index("rep")
        self.depth = fsdp // 2
        self.z, self.y, self.x, self.c = f // 2, f % 2, p // 2, p % 2

    def at(self, half, z, a=0, b=0, c=0):
        dy, dx = (a, b) if half == 0 else (b, a)
        return z, (self.y + dy) % 2, (self.x + dx) % 2, (self.c + c) % 2

    def index(self, *where):
        z, y, x, c = self.at(*where)
        return ((z * 2 + y) * 2 + x) * 2 + c

    def device(self, *where):
        z, y, x, c = self.at(*where)
        return z * 2 + y, x * 2 + c

    def turn(self, k):
        return (self.z + k) % self.depth

    def greet(self, barrier):
        def one(k, carry):
            signal(barrier, self.device(0, self.turn(k)))
            return carry

        lax.fori_loop(1, self.depth, one, 0)
        for flips in ((1, 0, 0), (0, 1, 0), (0, 0, 1)):
            signal(barrier, self.device(0, self.z, *flips))

    def wait_all(self, barrier):
        pl.semaphore_wait(barrier, self.depth + 2)


def signal(sem, device):
    pl.semaphore_signal(sem, inc=1, device_id=device, device_id_type=pl.DeviceIdType.MESH)


def remote(src, dst, send, recv, device):
    return pltpu.make_async_remote_copy(
        src_ref=src, dst_ref=dst, send_sem=send, recv_sem=recv,
        device_id=device, device_id_type=pl.DeviceIdType.MESH,
    )


def each(start, stop, body):
    def one(k, carry):
        body(k)
        return carry

    lax.fori_loop(start, stop, one, 0)


def own_share(
    first, mid, narrow, skip, last, cfirst, cmid, fg, fb, mg, mb, sg, sb, cg, cb, cmg, cmb, cl, wid
):
    d_first, d_narrow, d_last, d_cfirst = share_rows(first, narrow, last, cfirst, wid)

    def vec(ref, k=None):
        row = as_row(ref) if k is None else ref[...].astype(F32)[k : k + 1]
        return column(row)

    lane = iota((1, 128), 1)
    parts = [scaled_rows(mid[k].astype(F32), vec(mg, k)) for k in range(4)]
    parts.append(pltpu.roll(scaled_rows(skip[...].astype(F32), vec(sg)), ENC, 1))
    parts += [scaled_rows(cmid[k].astype(F32), vec(cmg, k)) for k in range(3)]
    s_cfirst = scaled_rows(d_cfirst, vec(cg))
    parts.append(pltpu.roll(s_cfirst, 384 - NX, 1)[:, 0:H])
    left = scaled_rows(d_first, vec(fg)) + jnp.where(lane == ENC, vec(fb), 0.0)
    right = jnp.where(lane < NX, s_cfirst[:, 0:128], 0.0) + jnp.where(lane == NX, vec(cb), 0.0)
    biases = [(1, mb, 0), (2, mb, 1), (3, mb, 2), (4, mb, 3), (5, sb, None), (7, cmb, 0), (8, cmb, 1), (9, cmb, 2)]
    for j, ref, k in biases:
        right = right + jnp.where(lane == BIASES - 128 + j, vec(ref, k), 0.0)
    right = right + jnp.where(lane == TAIL - 128, d_last[:, 0:1], 0.0)
    for c in range(3):
        right = right + jnp.where(lane == TAIL - 127 + c, vec(cl, c), 0.0)
    parts.append(jnp.concatenate([left, right], axis=1))
    parts.append(pltpu.roll(d_narrow, ENC, 1))
    parts.append(pltpu.roll(d_last, 383, 1)[:, 0:H])
    return jnp.concatenate(parts, axis=0).astype(BF)


def gather(place, out, send, recv, meanwhile):
    z, depth = place.z, place.depth
    me = place.index(0, z)
    rows = out.shape[1] // 2

    def copy(half, slab, s, *to):
        part = out.at[slab, pl.ds(half * rows, rows)]
        return remote(part, part, send.at[half, s], recv.at[half, slab], place.device(half, *to))

    def arrived(half, slab):
        copy(half, slab, 0, z, 0, 0, 1).wait_recv()

    def along_z(k):
        for half in range(2):
            copy(half, me, k - 1, place.turn(k)).start()

    def pass_on(half, slab, t, stage):
        base = depth - 1
        if stage == 0:
            copy(half, slab, base + t, z, 1).start()
        if stage <= 1:
            copy(half, slab, base + depth + 2 * t + stage, z, 0, 1).start()
        copy(half, slab, base + 3 * depth + 4 * t + stage, z, 0, 0, 1).start()

    each(1, depth, along_z)
    for half in range(2):
        pass_on(half, me, 0, 0)

    def from_z(k):
        for half in range(2):
            slab = place.index(half, place.turn(k))
            arrived(half, slab)
            pass_on(half, slab, k, 0)

    def from_a(k):
        for half in range(2):
            slab = place.index(half, place.turn(k), 1)
            arrived(half, slab)
            pass_on(half, slab, k, 1)

    def from_b(k):
        for half in range(2):
            slab = place.index(half, place.turn(k), 0, 1)
            arrived(half, slab)
            pass_on(half, slab, k, 2)

    def from_ab(k):
        for half in range(2):
            slab = place.index(half, place.turn(k), 1, 1)
            arrived(half, slab)
            pass_on(half, slab, k, 3)

    def from_core(k):
        for half in range(2):
            for a in range(2):
                for b in range(2):
                    arrived(half, place.index(half, place.turn(k), a, b, 1))

    def sent(s):
        for half in range(2):
            copy(half, me, s, z, 0, 0, 1).wait_send()

    meanwhile()
    each(1, depth, from_z)
    each(0, depth, from_a)
    each(0, depth, from_b)
    each(0, depth, from_ab)
    each(0, depth, from_core)
    each(0, 8 * depth - 1, sent)


def compute_kernel(
    fsdp, anch, dirs, delt, fore, cot, var, ng, nb, lg, lb, cg, cb, *rest
):
    layers, rest = rest[:18], rest[18:]
    compute_body(fsdp, layers, anch, dirs, delt, fore, cot, var, ng, nb, lg, lb, cg, cb, *rest)


def compute_body(
    fsdp, layers, anch, dirs, delt, fore, cot, var, ng, nb, lg, lb, cg, cb,
    rgb_o, ag_o, dg_o, deltag_o, gout, tot_o, inv_o, smalls,
    gathered, wid, send, recv, wts, sm, wt, w, wt7, w0t, w0, wcft, wcx, wclt, wcl, w7s, bb,
    enc, fe, xt, dep, cols,
    hx, ss, us, zg, ts, fx, hc, dc, zc, encb, dzb,
    de, nr, row7, rowc, dzr, dx, eb, outc,
    acc, acc0, accx, accl, vac,
):
    rays = delt.shape[0]
    lane128 = iota((1, 128), 1)

    place = Place(fsdp)
    barrier = pltpu.get_barrier_semaphore()
    place.greet(barrier)
    gathered[place.index(0, place.z)] = own_share(*layers, wid)
    place.wait_all(barrier)

    def meanwhile():
        cols[...] = jnp.zeros(cols.shape, F32)
        cols[0:3, 0:rays] = anch[...]
        cols[3:6, 0:rays] = dirs[...]
        cols[6:9, 0:rays] = cot[...]
        percol = cols[...].T
        cols[...] = percol
        low = (iota((SAMP, SAMP), 0) <= iota((SAMP, SAMP), 1)).astype(F32)
        dall = delt[...]
        depth = 0.1 + exact(dall, low) - 0.5 * dall
        dep[...] = depth
        enc[...] = jnp.zeros(enc.shape, F32)
        xt[...] = jnp.zeros(xt.shape, F32)
        enc[pl.ds(ENC, rays, stride=EROWS), :] = jnp.ones((rays, SAMP), F32)
        xt[pl.ds(NX, rays, stride=EROWS), :] = jnp.ones((rays, SAMP), F32)

        def put_enc(f, value):
            fe[f] = value
            enc[pl.ds(f, rays, stride=EROWS), :] = value

        for c in range(3):
            view = jnp.broadcast_to(percol[0:rays, 3 + c : 4 + c], (rays, SAMP))
            p = percol[0:rays, c : c + 1] + depth * view
            put_enc(c, p)
            xt[pl.ds(c, rays, stride=EROWS), :] = p
            sn, cs = jnp.sin(p), jnp.cos(p)
            for k in range(6):
                put_enc(3 + 6 * k + c, sn)
                put_enc(6 + 6 * k + c, cs)
                sn, cs = 2.0 * sn * cs, 1.0 - 2.0 * sn * sn
            xt[pl.ds(3 + c, rays, stride=EROWS), :] = view
            sn, cs = jnp.sin(view), jnp.cos(view)
            for k in range(4):
                xt[pl.ds(6 + 6 * k + c, rays, stride=EROWS), :] = sn
                xt[pl.ds(9 + 6 * k + c, rays, stride=EROWS), :] = cs
                sn, cs = 2.0 * sn * cs, 1.0 - 2.0 * sn * sn

        nr[...] = jnp.zeros(nr.shape, F32)
        eb[...] = jnp.zeros(eb.shape, F32)
        dzr[...] = jnp.zeros(dzr.shape, F32)
        acc[...] = jnp.zeros(acc.shape, F32)
        acc0[...] = jnp.zeros(acc0.shape, F32)
        accx[...] = jnp.zeros(accx.shape, F32)
        accl[...] = jnp.zeros(accl.shape, F32)
        vac[...] = jnp.zeros(vac.shape, F32)
        hx[:, H : H + 16, 0:PTS] = jnp.ones((7, 16, PTS), BF)
        hx[:, H : H + 16, PTS:] = jnp.zeros((7, 16, PTS), BF)
        dzb[:, PTS:] = jnp.where(iota((16, PTS), 0) == 0, 1.0, 0.0).astype(BF)
        hc[:, H : H + 16, :] = jnp.ones((4, 16, PTS), BF)

    gather(place, gathered, send, recv, meanwhile)

    lane256 = iota((1, H), 1)
    sm[...] = jnp.zeros(sm.shape, F32)
    for k, ref in enumerate((ng, nb, lg, lb, cg, cb)):
        sm[k : k + 1, 0 : ref.shape[0]] = as_row(ref)
    near = pltpu.roll(sm[:, 0:H], H - NARROW, 1)
    tail_row = []
    for k in (0, 1):
        t = jnp.where(lane256 == TAIL, sm[2 + k : 3 + k, 0:1], 0.0)
        for c in range(3):
            t = t + jnp.where(lane256 == TAIL + 1 + c, sm[4 + k : 5 + k, c : c + 1], 0.0)
        tail_row.append(t)
    smalls[...] = jnp.concatenate(
        [
            near[0:1],
            near[1:2] + jnp.where(lane256 < ENC, -1e4, 0.0),
            pltpu.roll(sm[...], 383, 1)[2:4, 0:H],
            tail_row[0],
            tail_row[1],
            jnp.broadcast_to(as_row(var), (1, H)),
            jnp.zeros((1, H), F32),
        ],
        axis=0,
    )
    r = H // gathered.shape[0]
    rp = gathered.shape[1] // GROUPS
    for q in range(GROUPS // 2):
        pair = gathered[:, 2 * rp * q : 2 * rp * (q + 1), :].astype(F32)
        wts[2 * q] = pair[:, 0:r].reshape(H, H).astype(BF)
        wts[2 * q + 1] = pair[:, rp : rp + r].reshape(H, H).astype(BF)

    unit = (iota((H, H), 0) == iota((H, H), 1)).astype(BF)

    def turned(x):
        return nt(unit, x)

    misc = wts[9].astype(F32)
    misct = turned(wts[9])
    for k, src in enumerate((0, 1, None, 4, 2, 3, 5, 6, 7)):
        if src is not None:
            wt[k] = wts[src]
            w[k] = turned(wts[src]).astype(BF)
    d3 = wts[10].astype(F32)
    inv3 = lax.rsqrt(jnp.sum(d3 * d3, axis=0, keepdims=True) + EPS)
    w3 = (d3 * (smalls[0:1, :] * inv3)).astype(BF)
    w[2] = w3
    wt[2] = turned(w3).astype(BF)
    d7 = wts[11].astype(F32)
    inv7 = lax.rsqrt(jnp.sum(d7 * d7, axis=0, keepdims=True) + EPS)
    w7 = (d7 * (smalls[2:3, :] * inv7)).astype(BF)
    w[9] = w7
    wt7[0:H] = turned(w7).astype(BF)
    w[10] = turned(wts[8]).astype(BF)
    invm = lax.rsqrt(jnp.sum(misc * misc, axis=0, keepdims=True) + EPS)
    tail = (misc * (smalls[4:5, :] * invm)).astype(BF)
    tailt = turned(tail)[TAIL : TAIL + 8]
    tail = tail.astype(F32)
    row8 = iota((8, H), 0)
    none8 = jnp.zeros((8, H), F32)
    wt7[H : H + 16] = jnp.concatenate([jnp.where(row8 == 0, tailt, 0.0), none8], axis=0).astype(BF)
    wclt[...] = jnp.concatenate(
        [jnp.where((row8 > 0) & (row8 < 4), tailt, 0.0), none8], axis=0
    ).astype(BF)
    only = jnp.where((lane256 > TAIL) & (lane256 < TAIL + 4), tail, 0.0)
    wcl[...] = pltpu.roll(only, H - TAIL, 1)[:, 0:16].astype(BF)
    w7s[...] = jnp.broadcast_to(tail[:, TAIL : TAIL + 1], (H, 128))
    w0t[...] = misc[:, 0:EROWS].astype(BF)
    w0[...] = misct[0:EROWS].astype(BF)
    wcx[...] = misct[CROSS : CROSS + EROWS].astype(BF)
    wcft[:, 0:H] = wts[8]
    wcft[:, H : H + EROWS] = misc[:, CROSS : CROSS + EROWS].astype(BF)
    for k, j in enumerate((1, 2, None, 5, 3, 4, None, 7, 8, 9)):
        if j is not None:
            bb[k] = jnp.broadcast_to(misc[:, BIASES + j : BIASES + j + 1], (H, 128))
    bb[2] = jnp.broadcast_to(column(smalls[1:2, :]), (H, 128))
    bb[6] = jnp.broadcast_to(column(smalls[3:4, :]), (H, 128))
    inv_o[...] = jnp.concatenate([inv3, inv3, inv7, inv7, invm, invm, invm, invm], axis=0)

    inv_s = jnp.exp(10.0 * smalls[6:7, 0:1])

    def chunk(i, carry):
        r0 = pl.multiple_of(i * RC, RC)
        e0 = pl.multiple_of(i * (RC * EROWS), 8)

        def sub(j):
            return slice(j * SUB, (j + 1) * SUB)

        def sub2(j):
            return slice(PTS + j * SUB, PTS + (j + 1) * SUB)

        def gather_rows(ref, base, j, count):
            start = base + j * RSUB * count
            if not isinstance(start, int):
                start = pl.multiple_of(start, 8)
                return jnp.concatenate(
                    [ref[pl.ds(pl.multiple_of(start + t * count, 8), count), :] for t in range(RSUB)],
                    axis=1,
                )
            return jnp.concatenate(
                [ref[start + t * count : start + (t + 1) * count, :] for t in range(RSUB)], axis=1
            )

        def spread_rows(ref, j, count, value):
            for t in range(RSUB):
                at = (j * RSUB + t) * count
                ref[at : at + count, :] = value[0:count, t * SAMP : (t + 1) * SAMP]

        def ray_row(ref, f, count):
            return ref[pl.ds(f, RC, stride=count), :]

        for j in range(NSUB):
            encb[:, sub(j)] = gather_rows(enc, e0, j, EROWS).astype(BF)
        for l in range(7):
            if l == 0:
                zz = nn(w0t[...], encb[:, 0:PTS])
            else:
                zz = nn(wt[l - 1], hx[l - 1, 0:H, 0:PTS])
            for j in range(NSUB):
                z = zz[:, sub(j)]
                if l > 0:
                    z = z + wide(bb[l - 1])
                h, s = sharp(z)
                ss[l, :, sub(j)] = s.astype(BF)
                if l == 3:
                    e = gather_rows(enc, e0, j, EROWS)
                    keep = iota((EROWS, 1), 0) < ENC
                    h = h.astype(F32)
                    h = ROOT_HALF * jnp.concatenate(
                        [h[0:EROWS] + jnp.where(keep, e, 0.0), h[EROWS:]], axis=0
                    )
                hx[l, 0:H, sub(j)] = h.astype(BF)
        zz = nn(wt7[...], hx[6, 0:H, 0:PTS])
        for j in range(NSUB):
            z = zz[:, sub(j)]
            fx[0:H, sub(j)] = (z[0:H] + wide(bb[6])).astype(BF)
            spread_rows(row7, j, 16, z[H : H + 16])

        for j in range(NSUB):
            zg[6, :, sub2(j)] = wide(w7s[...]).astype(BF) * ss[6, :, sub(j)]
        for l in range(6, 0, -1):
            uu = nn(w[l - 1], zg[l, :, PTS:])
            for j in range(NSUB):
                u = uu[:, sub(j)].astype(BF)
                if l == 4:
                    u = u.astype(F32) * ROOT_HALF
                    spread_rows(de, j, EROWS, u)
                    u = u.astype(BF)
                us[l - 1, :, sub(j)] = u
                zg[l - 1, :, sub2(j)] = u * ss[l - 1, :, sub(j)]
        dd = nn(w0[...], zg[0, :, PTS:]).astype(BF).astype(F32)
        for j in range(NSUB):
            d = dd[:, sub(j)]
            spread_rows(de, j, EROWS, d + gather_rows(de, 0, j, EROWS))

        def feature(f):
            return fe[f, pl.ds(r0, RC), :]

        dcol = [percol_ref_col(cols, r0, 3 + c) for c in range(3)]
        ccol = [percol_ref_col(cols, r0, 6 + c) for c in range(3)]
        normal = []
        for c in range(3):
            n = ray_row(de, c, EROWS)
            for k in range(6):
                n = n + 2.0**k * (
                    feature(6 + 6 * k + c) * ray_row(de, 3 + 6 * k + c, EROWS)
                    - feature(3 + 6 * k + c) * ray_row(de, 6 + 6 * k + c, EROWS)
                )
            normal.append(n)
            nr[pl.ds(30 + c, RC, stride=EROWS), :] = n

        delta = delt[pl.ds(r0, RC), :]
        front = fore[pl.ds(r0, RC), :].astype(F32)
        signed = ray_row(row7, 0, 16) + smalls[5:6, TAIL : TAIL + 1]
        cosine = dcol[0] * normal[0] + dcol[1] * normal[1] + dcol[2] * normal[2]
        slope = softplus(-10.0 * cosine) * -0.1
        slope_d = sigmoid(-10.0 * cosine)
        half = slope * delta * 0.5
        before = sigmoid((signed - half) * inv_s)
        after = sigmoid((signed + half) * inv_s)
        ratio = (before - after + 1e-05) / (before + 1e-05)
        ratio_d = front * (sigmoid(20.0 * ratio) - sigmoid(20.0 * (ratio - 1.0)))
        opacity = front * (softplus(20.0 * ratio) - softplus(20.0 * (ratio - 1.0))) * 0.05
        factor = 1.0 - opacity + 1e-07
        survive = factor
        lane = iota((RC, SAMP), 1)
        step = 1
        while step < SAMP:
            survive = survive * jnp.where(lane >= step, pltpu.roll(survive, step, 1), 1.0)
            step *= 2
        through = jnp.where(lane >= 1, pltpu.roll(survive, 1, 1), 1.0)
        contrib = opacity * through

        for j in range(NSUB):
            x = gather_rows(xt, e0, j, EROWS) + gather_rows(nr, 0, j, EROWS)
            fx[H : H + EROWS, sub(j)] = x.astype(BF)
        for l in range(4):
            if l == 0:
                zz = nn(wcft[...], fx[...])
            else:
                zz = nn(wt[5 + l], hc[l - 1, 0:H])
            for j in range(NSUB):
                z = zz[:, sub(j)]
                if l > 0:
                    z = z + wide(bb[6 + l])
                h, d = silu(z)
                hc[l, 0:H, sub(j)] = h.astype(BF)
                dc[l, :, sub(j)] = d.astype(BF)
        zz = nn(wclt[...], hc[3, 0:H])
        for j in range(NSUB):
            spread_rows(rowc, j, 16, zz[:, sub(j)])

        out = jnp.zeros((RC, 128), F32)
        dcontrib = jnp.zeros((RC, SAMP), F32)
        for c in range(3):
            color = sigmoid(ray_row(rowc, 1 + c, 16) + smalls[5:6, TAIL + 1 + c : TAIL + 2 + c])
            out = out + jnp.where(lane128 == c, jnp.sum(contrib * color, axis=1, keepdims=True), 0.0)
            dcontrib = dcontrib + ccol[c] * color
            dlogit = ccol[c] * contrib * color * (1.0 - color)
            dzr[pl.ds(1 + c, RC, stride=16), :] = dlogit
            vac[2 + c] += dlogit
        weighted = dcontrib * contrib
        after_sum = exact(weighted, (iota((SAMP, SAMP), 0) > iota((SAMP, SAMP), 1)).astype(F32))
        dratio = (dcontrib * through - after_sum / factor) * ratio_d
        base = 1.0 / (before + 1e-05)
        dbefore = dratio * after * base * base * before * (1.0 - before)
        dafter = -dratio * base * after * (1.0 - after)
        dsigned = (dbefore + dafter) * inv_s
        dhalf = (dafter - dbefore) * inv_s
        vac[0] += dbefore * (signed - half) + dafter * (signed + half)
        vac[1] += dsigned
        dzr[pl.ds(0, RC, stride=16), :] = dsigned
        ddelta = dhalf * slope * 0.5
        dcosine = dhalf * delta * 0.5 * slope_d
        for j in range(NSUB):
            dzb[:, sub(j)] = gather_rows(dzr, 0, j, 16).astype(BF)

        zc[3] = nn(wcl[...], dzb[:, 0:PTS]).astype(BF) * dc[3]
        for l in range(3, 0, -1):
            zc[l - 1] = nn(w[5 + l], zc[l]).astype(BF) * dc[l - 1]
            acc[5 + l] += nt(hc[l - 1], zc[l])
        dd = nn(wcx[...], zc[0]).astype(BF).astype(F32)
        for j in range(NSUB):
            spread_rows(dx, j, EROWS, dd[:, sub(j)])
        accx[...] += nt(fx[...], zc[0])
        accl[0] += nt(dzb[:, 0:PTS], hc[3, 0:H])
        fx[0:H] = nn(w[10], zc[0]).astype(BF)

        dpoint, dview = [], []
        for c in range(3):
            nb = ray_row(dx, 30 + c, EROWS) + dcosine * dcol[c]
            p = ray_row(dx, c, EROWS)
            v = ray_row(dx, 3 + c, EROWS) + dcosine * normal[c]
            eb[pl.ds(c, RC, stride=EROWS), :] = nb
            for k in range(6):
                two = 2.0**k
                sn, cs = feature(3 + 6 * k + c), feature(6 + 6 * k + c)
                eb[pl.ds(3 + 6 * k + c, RC, stride=EROWS), :] = two * cs * nb
                eb[pl.ds(6 + 6 * k + c, RC, stride=EROWS), :] = -two * sn * nb
                p = p - (two * two) * nb * (
                    sn * ray_row(de, 3 + 6 * k + c, EROWS) + cs * ray_row(de, 6 + 6 * k + c, EROWS)
                )
            for k in range(4):
                sn = xt[pl.ds(e0 + 6 + 6 * k + c, RC, stride=EROWS), :]
                cs = xt[pl.ds(e0 + 9 + 6 * k + c, RC, stride=EROWS), :]
                v = v + 2.0**k * (
                    cs * ray_row(dx, 6 + 6 * k + c, EROWS) - sn * ray_row(dx, 9 + 6 * k + c, EROWS)
                )
            dpoint.append(p)
            dview.append(v)

        for j in range(NSUB):
            encb[:, sub2(j)] = gather_rows(eb, 0, j, EROWS).astype(BF)
        for l in range(7):
            if l == 0:
                gg = nn(w0t[...], encb[:, PTS:])
            else:
                gg = nn(wt[l - 1], hx[l - 1, 0:H, PTS:])
            for j in range(NSUB):
                g = gg[:, sub(j)]
                s = ss[l, :, sub(j)]
                if l == 3:
                    g = g * s.astype(F32)
                    x = g.astype(BF)
                else:
                    x = g.astype(BF) * s
                u = wide(w7s[...]).astype(BF) if l == 6 else us[l, :, sub(j)]
                ts[l, :, sub(j)] = x * u * (2.0 - 2.0 * s)
                if l == 3:
                    e = gather_rows(eb, 0, j, EROWS)
                    x = ROOT_HALF * jnp.concatenate([g[0:EROWS] + e, g[EROWS:]], axis=0)
                    x = x.astype(BF)
                hx[l, 0:H, sub2(j)] = x

        dd = nn(w[9], fx[0:H])
        for j in range(NSUB):
            row = gather_rows(dzr, 0, j, 16)[0:1]
            d = dd[:, sub(j)] + wide(w7s[...]) * row
            zg[6, :, sub(j)] = d.astype(BF) * ss[6, :, sub(j)] + ts[6, :, sub(j)]
        acc[9] += nt(hx[6, :, 0:PTS], fx[0:H])
        accl[1] += nt(dzb[...], hx[6, 0:H])
        for l in range(6, 0, -1):
            dd = nn(w[l - 1], zg[l, :, 0:PTS])
            for j in range(NSUB):
                d = dd[:, sub(j)].astype(BF)
                if l == 4:
                    d = d.astype(F32) * ROOT_HALF
                    spread_rows(dx, j, EROWS, d)
                    d = d.astype(BF)
                zg[l - 1, :, sub(j)] = d * ss[l - 1, :, sub(j)] + ts[l - 1, :, sub(j)]
            acc[l - 1] += nt(hx[l - 1], zg[l])
        acc0[...] += nt(encb[...], zg[0])
        dd = nn(w0[...], zg[0, :, 0:PTS]).astype(BF).astype(F32)
        for j in range(NSUB):
            spread_rows(dx, j, EROWS, dd[:, sub(j)] + gather_rows(dx, 0, j, EROWS))

        depth = dep[pl.ds(r0, RC), :]
        ddepth = jnp.zeros((RC, SAMP), F32)
        for c in range(3):
            p = dpoint[c] + ray_row(dx, c, EROWS)
            for k in range(6):
                p = p + 2.0**k * (
                    feature(6 + 6 * k + c) * ray_row(dx, 3 + 6 * k + c, EROWS)
                    - feature(3 + 6 * k + c) * ray_row(dx, 6 + 6 * k + c, EROWS)
                )
            ddepth = ddepth + p * dcol[c]
            v = dview[c] + depth * p
            out = out + jnp.where(lane128 == 3 + c, jnp.sum(p, axis=1, keepdims=True), 0.0)
            out = out + jnp.where(lane128 == 6 + c, jnp.sum(v, axis=1, keepdims=True), 0.0)
        outc[pl.ds(r0, RC), :] = out
        later = exact(ddepth, (iota((SAMP, SAMP), 0) >= iota((SAMP, SAMP), 1)).astype(F32))
        deltag_o[pl.ds(r0, RC), :] = ddelta + later - 0.5 * ddepth
        return carry

    lax.fori_loop(0, rays // RC, chunk, 0)

    result = outc[...].T
    rgb_o[...] = result[0:3, 0:rays]
    ag_o[...] = result[3:6, 0:rays]
    dg_o[...] = result[6:9, 0:rays]
    tail_rows = jnp.where(row8 == 0, accl[1, 0:8], accl[0, 0:8])
    lines = [acc[0, H : H + 1]]
    for k in (0, 1, 4, 5, 3, 0, 6, 7, 8):
        lines.append(acc[k, H : H + 1])
    small_rows = jnp.concatenate(lines, axis=0)
    upper = jnp.concatenate(
        [
            acc0[...],
            jnp.zeros((CROSS - EROWS, H), F32),
            accx[H : H + EROWS],
            jnp.zeros((BIASES - CROSS - EROWS, H), F32),
            small_rows,
            jnp.zeros((TAIL - BIASES - 10, H), F32),
            tail_rows,
            jnp.zeros((H - TAIL - 8, H), F32),
        ],
        axis=0,
    )
    packed = turned(upper.astype(BF))
    groups = [turned(acc[k, 0:H].astype(BF)) for k in (0, 1, 4, 5, 3, 6, 7, 8)]
    groups += [turned(accx[0:H].astype(BF)), packed, acc[2, 0:H], acc[9, 0:H]]

    for q in range(GROUPS // 2):
        pair = [groups[2 * q + t].reshape(H // rp, rp, H) for t in range(2)]
        gout[:, 2 * rp * q : 2 * rp * (q + 1), :] = jnp.concatenate(pair, axis=1).astype(BF)

    def total(k):
        return jnp.sum(jnp.sum(vac[k], axis=1, keepdims=True), axis=0, keepdims=True)

    lane_bias = jnp.zeros((1, H), F32)
    for k in range(4):
        lane_bias = lane_bias + jnp.where(lane256 == TAIL + k, total(1 + k), 0.0)
    variance = jnp.where(lane256 == 0, total(0) * inv_s * 10.0, 0.0)
    tot_o[...] = jnp.concatenate(
        [
            jnp.sum(d3 * acc[2, 0:H], axis=0, keepdims=True),
            acc[2, H : H + 1],
            jnp.sum(d7 * acc[9, 0:H], axis=0, keepdims=True),
            acc[9, H : H + 1],
            jnp.sum(misc * packed, axis=0, keepdims=True),
            lane_bias,
            variance,
            jnp.zeros((1, H), F32),
        ],
        axis=0,
    )


def percol_ref_col(ref, r0, j):
    return jnp.broadcast_to(ref[pl.ds(r0, RC), j : j + 1], (RC, SAMP))


def compute(fsdp, devices, anchors, directions, deltas, foreground, cotangent, smalls, layers):
    rays = deltas.shape[0]
    vm, dma = pltpu.VMEM, pltpu.SemaphoreType.DMA
    rp = layers[0].shape[0]
    points = rays * EROWS
    scratch = [
        vm((devices, GROUPS * rp, H), BF),
        vm((4, rp, 384), F32),
        dma((2, devices)),
        dma((2, devices)),
        vm((GROUPS, H, H), BF),
        vm((8, 384), F32),
        vm((9, H, H), BF),
        vm((11, H, H), BF),
        vm((H + 16, H), BF),
        vm((H, EROWS), BF),
        vm((EROWS, H), BF),
        vm((H, H + EROWS), BF),
        vm((EROWS, H), BF),
        vm((16, H), BF),
        vm((H, 16), BF),
        vm((H, 128), F32),
        vm((10, H, 128), F32),
        vm((points, SAMP), F32),
        vm((ENC, rays, SAMP), F32),
        vm((points, SAMP), F32),
        vm((rays, SAMP), F32),
        vm((128, 128), F32),
        vm((7, H + 16, 2 * PTS), BF),
        vm((7, H, PTS), BF),
        vm((6, H, PTS), BF),
        vm((7, H, 2 * PTS), BF),
        vm((7, H, PTS), BF),
        vm((H + EROWS, PTS), BF),
        vm((4, H + 16, PTS), BF),
        vm((4, H, PTS), BF),
        vm((4, H, PTS), BF),
        vm((EROWS, 2 * PTS), BF),
        vm((16, 2 * PTS), BF),
        vm((RC * EROWS, SAMP), F32),
        vm((RC * EROWS, SAMP), F32),
        vm((RC * 16, SAMP), F32),
        vm((RC * 16, SAMP), F32),
        vm((RC * 16, SAMP), F32),
        vm((RC * EROWS, SAMP), F32),
        vm((RC * EROWS, SAMP), F32),
        vm((128, 128), F32),
        vm((10, H + 16, H), F32),
        vm((EROWS, H), F32),
        vm((H + EROWS, H), F32),
        vm((2, 16, H), F32),
        vm((5, RC, SAMP), F32),
    ]
    shapes = (
        jax.ShapeDtypeStruct((3, rays), F32),
        jax.ShapeDtypeStruct((3, rays), F32),
        jax.ShapeDtypeStruct((3, rays), F32),
        jax.ShapeDtypeStruct((rays, SAMP), F32),
        jax.ShapeDtypeStruct((H // rp, GROUPS * rp, H), BF),
        jax.ShapeDtypeStruct((8, H), F32),
        jax.ShapeDtypeStruct((8, H), F32),
        jax.ShapeDtypeStruct((8, H), F32),
    )
    whole = pl.BlockSpec(memory_space=pltpu.VMEM)
    return pl.pallas_call(
        functools.partial(compute_kernel, fsdp),
        out_shape=shapes,
        in_specs=[whole] * 30,
        out_specs=(whole,) * 8,
        scratch_shapes=scratch,
        name="nets",
        compiler_params=pltpu.CompilerParams(
            collective_id=0, has_side_effects=True, vmem_limit_bytes=62 * 1024 * 1024
        ),
    )(anchors, directions, deltas, foreground, cotangent, *smalls, *layers)


def scatter_kernel(fsdp, g, tot, share, tot_o, rcc, rca, rcb, rcz, tc, ta, tb, tz, send, sc, sa, sb, sz, tsend, trecv):
    place = Place(fsdp)
    z, depth = place.z, place.depth
    barrier = pltpu.get_barrier_semaphore()
    place.greet(barrier)
    place.wait_all(barrier)
    rows = g.shape[1] // 2

    def own(half, k, a, b, c):
        return g.at[place.index(half, place.turn(k), a, b, c), pl.ds(half * rows, rows)]

    def add(x, y):
        return x[...].astype(F32) + y[...].astype(F32)

    def to_core(half, k, a, b):
        slot = k * 4 + a * 2 + b
        return remote(
            own(half, k, a, b, 1), rcc.at[half, slot], send.at[half, slot], sc.at[half, slot],
            place.device(half, z, 0, 0, 1),
        )

    def to_a(half, k, b):
        slot = k * 2 + b
        return remote(
            rcc.at[half, k * 4 + 2 + b], rca.at[half, slot], send.at[half, 4 * depth + slot],
            sa.at[half, slot], place.device(half, z, 1),
        )

    def to_b(half, k):
        return remote(
            rca.at[half, k * 2 + 1], rcb.at[half, k], send.at[half, 6 * depth + k], sb.at[half, k],
            place.device(half, z, 0, 1),
        )

    def to_z(half, k):
        return remote(
            rcb.at[half, k], rcz.at[half, k], send.at[half, 7 * depth + k], sz.at[half, k],
            place.device(half, place.turn(k)),
        )

    def tot_copy(src, dst, k, *to):
        return remote(src, dst, tsend.at[k], trecv.at[k], place.device(0, *to))

    def order(body):
        each(1, depth, body)
        body(0)

    t_core = tot_copy(tot, tc, 0, z, 0, 0, 1)
    t_core.start()
    for a, b in ((1, 1), (1, 0), (0, 1), (0, 0)):

        def start_core(k):
            for half in range(2):
                to_core(half, k, a, b).start()

        order(start_core)

    def join_core(k, a, b):
        for half in range(2):
            slot = k * 4 + a * 2 + b
            to_core(half, k, a, b).wait_recv()
            rcc[half, slot] = add(rcc.at[half, slot], own(half, k, a, b, 0)).astype(BF)
            if a:
                to_a(half, k, b).start()

    order(lambda k: join_core(k, 1, 1))
    order(lambda k: join_core(k, 1, 0))
    t_core.wait()
    tc[...] = tot[...] + tc[...]
    t_a = tot_copy(tc, ta, 1, z, 1)
    t_a.start()
    order(lambda k: join_core(k, 0, 1))
    order(lambda k: join_core(k, 0, 0))
    t_a.wait()
    ta[...] = tc[...] + ta[...]
    t_b = tot_copy(ta, tb, 2, z, 0, 1)
    t_b.start()

    def join_a(k, b):
        for half in range(2):
            slot = k * 2 + b
            to_a(half, k, b).wait_recv()
            rca[half, slot] = add(rca.at[half, slot], rcc.at[half, k * 4 + b]).astype(BF)
            if b:
                to_b(half, k).start()

    order(lambda k: join_a(k, 1))
    t_b.wait()
    tz[z] = ta[...] + tb[...]

    def start_tot(k):
        tot_copy(tz.at[z], tz.at[z], 2 + k, place.turn(k)).start()

    each(1, depth, start_tot)
    order(lambda k: join_a(k, 0))

    def join_b(k):
        for half in range(2):
            to_b(half, k).wait_recv()
            rcb[half, k] = add(rcb.at[half, k], rca.at[half, k * 2]).astype(BF)
            to_z(half, k).start()

    each(1, depth, join_b)
    for half in range(2):
        to_b(half, 0).wait_recv()
        share[half * rows : (half + 1) * rows] = add(rcb.at[half, 0], rca.at[half, 0])

    def join_z(k):
        for half in range(2):
            to_z(half, k).wait_recv()
            share[half * rows : (half + 1) * rows] += rcz[half, k].astype(F32)

    each(1, depth, join_z)

    def end_tot(k):
        tot_copy(tz.at[z], tz.at[z], 2 + k, place.turn(k)).wait()

    each(1, depth, end_tot)
    total = tz[0]
    for k in range(1, depth):
        total = total + tz[k]
    tot_o[...] = total

    def sent(k):
        for half in range(2):
            for a in range(2):
                for b in range(2):
                    to_core(half, k, a, b).wait_send()
            to_a(half, k, 0).wait_send()
            to_a(half, k, 1).wait_send()
            to_b(half, k).wait_send()

    each(0, depth, sent)

    def sent_z(k):
        for half in range(2):
            to_z(half, k).wait_send()

    each(1, depth, sent_z)


def unscaled_rows(d, gain, grad):
    inv = lax.rsqrt(jnp.sum(d * d, axis=1, keepdims=True) + EPS)
    dot = jnp.sum(d * grad, axis=1, keepdims=True)
    return grad * (gain * inv) - d * (gain * inv * inv * inv * dot), dot * inv


def finish_kernel(
    share, tot, inv, smalls, first, mid, narrow, skip, last, cfirst, cmid,
    fg, mg, sg, cg, cmg, cl, rgb, ag, dg, deltag, o_rgb, o_ag, o_dg, o_deltag,
    o_first, o_fg, o_fb, o_mid, o_mg, o_mb, o_narrow, o_ng, o_nb, o_skip, o_sg, o_sb,
    o_last, o_lg, o_lb, o_cfirst, o_cg, o_cb, o_cmid, o_cmg, o_cmb, o_clast, o_clg, o_clb, o_var,
    wid,
):
    r = first.shape[0]
    for src, dst in ((rgb, o_rgb), (ag, o_ag), (dg, o_dg), (deltag, o_deltag)):
        dst[...] = src[...]
    d_first, d_narrow, d_last, d_cfirst = share_rows(first, narrow, last, cfirst, wid)

    def vec(ref, k=None):
        return column(as_row(ref) if k is None else ref[...].astype(F32)[k : k + 1])

    def group(k):
        return share[k * r : (k + 1) * r, :]

    def put(ref, col):
        ref[...] = line(col).reshape(r)

    def put_rows(ref, columns):
        ref[...] = jnp.concatenate([line(col) for col in columns], axis=0)

    misc = group(9)
    lane = iota((1, 128), 1)
    g, gain = unscaled_rows(d_first, vec(fg), jnp.where(lane < ENC, misc[:, 0:128], 0.0))
    o_first[...] = g[:, 0:ENC]
    put(o_fg, gain)
    put(o_fb, misc[:, ENC : ENC + 1])
    gains = []
    for k in range(4):
        g, gain = unscaled_rows(mid[k].astype(F32), vec(mg, k), group(k))
        o_mid[k] = g
        gains.append(gain)
    put_rows(o_mg, gains)
    put_rows(o_mb, [misc[:, BIASES + 1 + k : BIASES + 2 + k] for k in range(4)])
    g, gain = unscaled_rows(skip[...].astype(F32), vec(sg), pltpu.roll(group(4), H - ENC, 1))
    o_skip[...] = g
    put(o_sg, gain)
    put(o_sb, misc[:, BIASES + 5 : BIASES + 6])
    extra = jnp.where(lane < NX, misc[:, 128:256], 0.0)
    moved = jnp.concatenate([group(8), jnp.zeros((r, 128), F32)], axis=1)
    grad = pltpu.roll(moved, NX, 1) + jnp.concatenate([extra, jnp.zeros((r, H), F32)], axis=1)
    g, gain = unscaled_rows(d_cfirst, vec(cg), grad)
    o_cfirst[...] = g[:, 0 : H + NX]
    put(o_cg, gain)
    put(o_cb, misc[:, CROSS + NX : CROSS + NX + 1])
    gains = []
    for k in range(3):
        g, gain = unscaled_rows(cmid[k].astype(F32), vec(cmg, k), group(5 + k))
        o_cmid[k] = g
        gains.append(gain)
    put_rows(o_cmg, gains)
    put_rows(o_cmb, [misc[:, BIASES + 7 + k : BIASES + 8 + k] for k in range(3)])

    def across(k, d, grad):
        gain, iv, dot = smalls[k : k + 1, :], inv[k : k + 1, :], tot[k : k + 1, :]
        return grad * (gain * iv) - d * (gain * iv * iv * iv * dot)

    g = across(0, pltpu.roll(d_narrow, ENC, 1), group(10))
    o_narrow[...] = pltpu.roll(g, H - ENC, 1)[:, 0:NARROW]
    g = across(2, pltpu.roll(d_last, 383, 1)[:, 0:H], group(11))
    right = jnp.where(lane == TAIL - 128, d_last[:, 0:1], 0.0)
    for c in range(3):
        right = right + jnp.where(lane == TAIL - 127 + c, vec(cl, c), 0.0)
    t = across(4, jnp.concatenate([jnp.zeros((r, 128), F32), right], axis=1), misc)
    first_lane = iota((1, 384), 1) == 0

    def behind(x, front):
        more = jnp.zeros((x.shape[0], 128), F32)
        moved = pltpu.roll(jnp.concatenate([x, more], axis=1), 1, 1)
        return jnp.where(first_lane, front, moved)[:, 0 : H + 1]

    o_last[...] = behind(g, t[:, TAIL : TAIL + 1])
    put_rows(o_clast, [t[:, TAIL + 1 + c : TAIL + 2 + c] for c in range(3)])
    gained = tot[...] * inv[...]
    back = pltpu.roll(jnp.concatenate([gained[0:1], tot[1:2], jnp.zeros((6, H), F32)], axis=0), H - ENC, 1)
    o_ng[...] = back[0:1, 0:NARROW].reshape(NARROW)
    o_nb[...] = back[1:2, 0:NARROW].reshape(NARROW)
    eight = jnp.zeros((7, H), F32)
    o_lg[...] = behind(jnp.concatenate([gained[2:3], eight], axis=0), gained[4:5, TAIL : TAIL + 1])[0:1].reshape(H + 1)
    o_lb[...] = behind(jnp.concatenate([tot[3:4], eight], axis=0), tot[5:6, TAIL : TAIL + 1])[0:1].reshape(H + 1)
    tails = jnp.concatenate([gained[4:5], tot[5:6], jnp.zeros((6, H), F32)], axis=0)
    tails = pltpu.roll(tails, H - TAIL - 1, 1)
    o_clg[...] = tails[0:1, 0:3].reshape(3)
    o_clb[...] = tails[1:2, 0:3].reshape(3)
    o_var[...] = tot[6:7, 0:1].reshape(1)


def per_device(
    fsdp, devices,
    anchors, directions, deltas, foreground,
    sdf_first_dir, sdf_first_gain, sdf_first_bias,
    sdf_mid_dir, sdf_mid_gain, sdf_mid_bias,
    sdf_narrow_dir, sdf_narrow_gain, sdf_narrow_bias,
    sdf_skip_dir, sdf_skip_gain, sdf_skip_bias,
    sdf_last_dir, sdf_last_gain, sdf_last_bias,
    color_first_dir, color_first_gain, color_first_bias,
    color_mid_dir, color_mid_gain, color_mid_bias,
    color_last_dir, color_last_gain, color_last_bias,
    variance, rgb_cotangent,
):
    r = sdf_first_gain.shape[0]
    rp = max(r, 8)
    depth = fsdp // 2
    whole = pl.BlockSpec(memory_space=pltpu.VMEM)
    vm, dma = pltpu.VMEM, pltpu.SemaphoreType.DMA

    def rows(x):
        return x if rp == r else jnp.pad(x, [(0, 0)] * (x.ndim - 2) + [(0, rp - r), (0, 0)])

    def lanes(x):
        return x if rp == r else jnp.pad(x, [(0, 0)] * (x.ndim - 1) + [(0, rp - r)])

    shares = (
        rows(sdf_first_dir.T),
        rows(jnp.swapaxes(sdf_mid_dir, 1, 2)),
        rows(sdf_narrow_dir),
        rows(sdf_skip_dir.T),
        rows(sdf_last_dir),
        rows(color_first_dir.T),
        rows(jnp.swapaxes(color_mid_dir, 1, 2)),
    )
    fg, fb, mg, mb, sg, sb, cg, cb, cmg, cmb, cl = (
        lanes(x)
        for x in (
            sdf_first_gain, sdf_first_bias, sdf_mid_gain, sdf_mid_bias, sdf_skip_gain, sdf_skip_bias,
            color_first_gain, color_first_bias, color_mid_gain, color_mid_bias, color_last_dir.T,
        )
    )
    size = GROUPS * rp
    limit = 60 * 1024 * 1024
    blocks = H // rp

    def ungroup(x):
        if rp == r:
            return x
        x = x.reshape(blocks, GROUPS, devices // blocks, r, H).transpose(0, 2, 1, 3, 4)
        return rows(x).reshape(devices, size, H)

    rgb, ag, dg, deltag, gout, tot, inv, smalls = compute(
        fsdp, devices, anchors, directions, deltas, foreground, rgb_cotangent,
        (
            variance, sdf_narrow_gain, sdf_narrow_bias, sdf_last_gain, sdf_last_bias,
            color_last_gain, color_last_bias,
        ),
        (*shares, fg, fb, mg, mb, sg, sb, cg, cb, cmg, cmb, cl),
    )
    half = size // 2
    share, tot = pl.pallas_call(
        functools.partial(scatter_kernel, fsdp),
        out_shape=(jax.ShapeDtypeStruct((size, H), F32), jax.ShapeDtypeStruct((8, H), F32)),
        in_specs=[whole] * 2,
        out_specs=(whole,) * 2,
        scratch_shapes=[
            vm((2, 4 * depth, half, H), BF),
            vm((2, 2 * depth, half, H), BF),
            vm((2, depth, half, H), BF),
            vm((2, depth, half, H), BF),
            vm((8, H), F32),
            vm((8, H), F32),
            vm((8, H), F32),
            vm((depth, 8, H), F32),
            dma((2, 8 * depth)),
            dma((2, 4 * depth)),
            dma((2, 2 * depth)),
            dma((2, depth)),
            dma((2, depth)),
            dma((2 + depth,)),
            dma((2 + depth,)),
        ],
        name="scatter",
        compiler_params=pltpu.CompilerParams(
            collective_id=1, has_side_effects=True, vmem_limit_bytes=limit
        ),
    )(ungroup(gout), tot)

    def f32(*shape):
        return jax.ShapeDtypeStruct(shape, F32)

    outs = pl.pallas_call(
        finish_kernel,
        out_shape=(
            f32(*rgb.shape), f32(*ag.shape), f32(*dg.shape), f32(*deltag.shape),
            f32(rp, ENC), f32(rp), f32(rp),
            f32(4, rp, H), f32(4, rp), f32(4, rp),
            f32(rp, NARROW), f32(NARROW), f32(NARROW),
            f32(rp, H), f32(rp), f32(rp),
            f32(rp, H + 1), f32(H + 1), f32(H + 1),
            f32(rp, H + NX), f32(rp), f32(rp),
            f32(3, rp, H), f32(3, rp), f32(3, rp),
            f32(3, rp), f32(3), f32(3),
            f32(1),
        ),
        in_specs=[whole] * 21,
        out_specs=(whole,) * 29,
        scratch_shapes=[vm((4, rp, 384), F32)],
        name="finish",
    )(share, tot, inv, smalls, *shares, fg, mg, sg, cg, cmg, cl, rgb, ag, dg, deltag)
    (
        rgb, ag, dg, deltag,
        o_first, o_fg, o_fb, o_mid, o_mg, o_mb, o_narrow, o_ng, o_nb, o_skip, o_sg, o_sb,
        o_last, o_lg, o_lb, o_cfirst, o_cg, o_cb, o_cmid, o_cmg, o_cmb, o_clast, o_clg, o_clb, o_var,
    ) = outs
    return (
        rgb, ag, dg, deltag,
        o_first[0:r].T, o_fg[0:r], o_fb[0:r],
        jnp.swapaxes(o_mid[:, 0:r], 1, 2), o_mg[:, 0:r], o_mb[:, 0:r],
        o_narrow[0:r], o_ng, o_nb,
        o_skip[0:r].T, o_sg[0:r], o_sb[0:r],
        o_last[0:r], o_lg, o_lb,
        o_cfirst[0:r].T, o_cg[0:r], o_cb[0:r],
        jnp.swapaxes(o_cmid[:, 0:r], 1, 2), o_cmg[:, 0:r], o_cmb[:, 0:r],
        o_clast[:, 0:r].T, o_clg, o_clb,
        o_var,
    )


def solution(mesh):
    fsdp, rep = mesh.shape["fsdp"], mesh.shape["rep"]
    assert rep == 4 and fsdp % 2 == 0
    both = ("fsdp", "rep")
    cols, vec, cols3, rows, copied = P(None, both), P(both), P(None, None, both), P(both, None), P()
    layers = (
        cols, vec, vec, cols3, cols, cols, rows, copied, copied, cols, vec, vec,
        rows, copied, copied, cols, vec, vec, cols3, cols, cols, rows, copied, copied,
    )
    return jax.shard_map(
        functools.partial(per_device, fsdp, fsdp * rep),
        mesh=mesh,
        in_specs=(cols, cols, rows, rows) + layers + (copied, cols),
        out_specs=(cols, cols, cols, rows) + layers + (copied,),
        check_vma=False,
    )
```

time: 1280 us -> 99.6 us (0.08)
  blocking collectives: 538 us -> 0 us
  waiting for transfers between devices: 285 us -> 0 us
  matrix products: 236 us -> 0 us
  local copies, waits for them, and re-layouts: 126 us -> 0 us
  Pallas kernels: 0 us -> 97.8 us
  other arithmetic: 66.8 us -> 0 us
  between operations: 20.6 us -> 1.5 us
    all_gather x12 -> x0, blocking collectives: 456 us -> none  [the longest x1 40.5 us: per_device(): lax.all_gather(sdf_mid_gain, ('fsdp', 'rep'), axis=1, tiled=True)]
    unnamed x6 -> x0, waiting for transfers between devices: 285 us -> none
    dot_general x62 -> x0, matrix products: 236 us -> none  [project(): jnp.dot(rows.astype(jnp.bfloat16), weight.astype(jnp.bfloat16), preferred...]
    pallas_call x0 -> x3, Pallas kernels: none -> 97.8 us  [the longest x1 74.3 us: compute(): pl.pallas_call(functools.partial(compute_kernel, fsdp), out_shape=shapes,...]
    unnamed x2 -> x0, blocking collectives: 82 us -> none
    concatenate x5 -> x0, local copies, waits for them, and re-layouts: 61.2 us -> none  [the longest x2 42.8 us: sdf_net(): hidden = jnp.concatenate([hidden, encoded], axis=1) * root_half]
    unnamed x655 -> x0, local copies, waits for them, and re-layouts: 41.3 us -> none
    reduce_sum x16 -> x0, other arithmetic: 23.3 us -> none  [the longest x2 8.75 us: project(): jnp.dot(rows.astype(jnp.bfloat16), weight.astype(jnp.bfloat16), preferred...]
  transfers between devices with their start and end apart: 3 -> 0, of which waited for: 3 -> 0; matrix products, arithmetic and copies ran while one was open for 6% -> 0% of each run, Pallas kernels for 0% -> 0%
where the time goes in v1:
time: 99.6 us; the launch traced here: 99.3 us
  Pallas kernels  97.8 us (98%)
  between operations  1.5 us (2%)
    pallas_call x1, Pallas kernels, compute(): pl.pallas_call(functools.partial(compute_kernel, fsdp), out_shape=shapes,...  74.3 us
    pallas_call x1, Pallas kernels, per_device(): pl.pallas_call(functools.partial(scatter_kernel, fsdp), out_shape=(jax.Sh...  21.4 us
    pallas_call x1, Pallas kernels, per_device(): pl.pallas_call(finish_kernel, out_shape=(f32(*rgb.shape), f32(*ag.shape),...  2.2 us

profile of v1, /device:TPU:0, one launch (start us, length us, event | category | flops | bytes accessed | tf_op | source)
XLA Modules:
  0.0 99.3 jit_solution(13085967222336085820)
XLA Ops:
  1.3 74.3 %nets.1 = (f32[3,32]{1,0:T(4,128)}, f32[3,32]{1,0:T(4,128)}, f32[3,32]{1,0:T(4,128)}, f32[32,128]{1,0:T(8,128)}, bf16[32,96,256]{2,1,0:T(8,128)(2,1)}, /*index=5...) custom-call(f32[3,32]{1,0:T(4,128)} %anch.1, f32[3,32]{1,0:T(4,128)} %dirs.1, f32[32,128]{1,0:T(8,128)} %delt.1, ...), custom_call_target="tpu_custom_call" | custom-call | tf_op jit(solution)/shard_map/nets/pallas_call | solution.py:788
  75.6 21.4 %scatter.1 = (f32[96,256]{1,0:T(8,128)}, f32[8,256]{1,0:T(8,128)}) custom-call(bf16[32,96,256]{2,1,0:T(8,128)(2,1)} %get-tuple-element.68.g, f32[8,256]{1,0:T(8,128)} %get-tuple-element.69.tot), custom_call_target="tpu_custom_call" | custom-call | tf_op jit(solution)/shard_map/scatter/pallas_call | solution.py:1098
  97.0 2.2 %finish.1 = (f32[3,32]{1,0:T(4,128)}, f32[3,32]{1,0:T(4,128)}, f32[3,32]{1,0:T(4,128)}, f32[32,128]{1,0:T(8,128)}, f32[8,39]{1,0:T(8,128)}, /*index=5*/f32[8]{0:...) custom-call(f32[96,256]{1,0:T(8,128)} %get-tuple-element.70.share, ...), custom_call_target="tpu_custom_call" | custom-call | tf_op jit(solution)/shard_map/finish/pallas_call | solution.py:1129

commit v2 on v1

--- a/solution.py
+++ b/solution.py
@@ -17,9 +17,7 @@
 NX = 33
 GROUPS = 12
 SUB = 256
-RC = 8
-PTS = RC * SAMP
-NSUB = PTS // SUB
+PAIRS = ((6, 7), (5, 8), (11, 3), (2, 4), (10, 1), (0, 9))
 RSUB = SUB // SAMP
 CROSS = 128
 BIASES = 200
@@ -180,16 +178,14 @@
     parts.append(jnp.concatenate([left, right], axis=1))
     parts.append(pltpu.roll(d_narrow, ENC, 1))
     parts.append(pltpu.roll(d_last, 383, 1)[:, 0:H])
-    return jnp.concatenate(parts, axis=0).astype(BF)
+    return [jnp.concatenate([parts[k] for k in pair], axis=0).astype(BF) for pair in PAIRS]
 
 
 def gather(place, out, send, recv, meanwhile):
     z, depth = place.z, place.depth
     me = place.index(0, z)
-    rows = out.shape[1] // 2
-
     def copy(half, slab, s, *to):
-        part = out.at[slab, pl.ds(half * rows, rows)]
+        part = out.at[pl.ds(half * 3, 3), slab]
         return remote(part, part, send.at[half, s], recv.at[half, slab], place.device(half, *to))
 
     def arrived(half, slab):
@@ -254,29 +250,176 @@
     each(0, 8 * depth - 1, sent)
 
 
+class Reduction:
+    def __init__(self, place, g, share, rcc, rca, rcb, rcz, send, sc, sa, sb, sz):
+        self.place, self.g, self.share = place, g, share
+        self.rcc, self.rca, self.rcb, self.rcz = rcc, rca, rcb, rcz
+        self.send, self.sc, self.sa, self.sb, self.sz = send, sc, sa, sb, sz
+
+    def side(self, q):
+        place = self.place
+        return (place.y, place.x) if q % 2 == 0 else (place.x, place.y)
+
+    def to_core(self, q, t):
+        n, place = 2 * self.place.depth, self.place
+        at = ((place.c + 1) % 2) * 2 + (self.side(q)[0] + t) % 2
+        return remote(
+            self.g.at[q, pl.ds(at * n, n)], self.rcc.at[q, t], self.send.at[q, t], self.sc.at[q, t],
+            place.device(q % 2, place.z, 0, 0, 1),
+        )
+
+    def to_a(self, q):
+        return remote(
+            self.rcc.at[q, 1], self.rca.at[q], self.send.at[q, 2], self.sa.at[q],
+            self.place.device(q % 2, self.place.z, 1),
+        )
+
+    def to_b(self, q):
+        n = self.place.depth
+        at = (self.side(q)[1] + 1) % 2
+        return remote(
+            self.rca.at[q, pl.ds(at * n, n)], self.rcb.at[q], self.send.at[q, 3], self.sb.at[q],
+            self.place.device(q % 2, self.place.z, 0, 1),
+        )
+
+    def to_z(self, q, k):
+        to = self.place.turn(k)
+        return remote(
+            self.rcb.at[q, to], self.rcz.at[q, k], self.send.at[q, 3 + k], self.sz.at[q, k],
+            self.place.device(0, to),
+        )
+
+    def begin(self, q, first, second):
+        depth = self.place.depth
+        count = depth * 8
+        r, rp = H // count, self.g.shape[2] // 2
+        for d in range(count):
+            z, y, x, c = d // 8, d // 4 % 2, d // 2 % 2, d % 2
+            a, b = (y, x) if q % 2 == 0 else (x, y)
+            parts = []
+            for m in (first, second):
+                parts.append(m[d * r : (d + 1) * r])
+                if rp > r:
+                    parts.append(jnp.zeros((rp - r, H), F32))
+            self.g[q, ((c * 2 + a) * 2 + b) * depth + z] = jnp.concatenate(parts, axis=0).astype(BF)
+        self.to_core(q, 1).start()
+        self.to_core(q, 0).start()
+
+    def own(self, q, t):
+        n = 2 * self.place.depth
+        return self.g[q, pl.ds((self.place.c * 2 + (self.side(q)[0] + t) % 2) * n, n)].astype(F32)
+
+    def step_a(self, q):
+        self.to_core(q, 1).wait_recv()
+        self.rcc[q, 1] = (self.rcc[q, 1].astype(F32) + self.own(q, 1)).astype(BF)
+        self.to_a(q).start()
+        self.to_core(q, 0).wait_recv()
+        self.rcc[q, 0] = (self.rcc[q, 0].astype(F32) + self.own(q, 0)).astype(BF)
+
+    def add_a(self, q, t):
+        n = self.place.depth
+        at = pl.ds(((self.side(q)[1] + t) % 2) * n, n)
+        self.rca[q, at] = (self.rca[q, at].astype(F32) + self.rcc[q, 0, at].astype(F32)).astype(BF)
+
+    def step_b(self, q):
+        self.to_a(q).wait_recv()
+        self.add_a(q, 1)
+        self.to_b(q).start()
+        self.add_a(q, 0)
+
+    def step_z(self, q):
+        n, z = self.place.depth, self.place.z
+        self.to_b(q).wait_recv()
+        at = pl.ds(self.side(q)[1] * n, n)
+        self.rcb[q] = (self.rcb[q].astype(F32) + self.rca[q, at].astype(F32)).astype(BF)
+        each(1, n, lambda k: self.to_z(q, k).start())
+        rows = self.g.shape[2]
+        self.share[q * rows : (q + 1) * rows] = self.rcb[q, z].astype(F32)
+
+    def step_end(self, q):
+        rows = self.g.shape[2]
+
+        def one(k):
+            self.to_z(q, k).wait_recv()
+            self.share[q * rows : (q + 1) * rows] += self.rcz[q, k].astype(F32)
+
+        each(1, self.place.depth, one)
+
+    def settle(self, q):
+        for t in range(2):
+            self.to_core(q, t).wait_send()
+        self.to_a(q).wait_send()
+        self.to_b(q).wait_send()
+        each(1, self.place.depth, lambda k: self.to_z(q, k).wait_send())
+
+
+class Total:
+    def __init__(self, place, tc, ta, tb, tz, own, send, recv):
+        self.place, self.bufs, self.own = place, (tc, ta, tb), own
+        self.tz, self.send, self.recv = tz, send, recv
+
+    def step(self, k):
+        to = ((0, 0, 1), (1, 0, 0), (0, 1, 0))[k]
+        return remote(
+            self.own.at[k], self.bufs[k], self.send.at[k], self.recv.at[k],
+            self.place.device(0, self.place.z, *to),
+        )
+
+    def begin(self, value):
+        self.own[0] = value
+        self.step(0).start()
+
+    def go_on(self, k):
+        self.step(k).wait()
+        value = self.own[k] + self.bufs[k][...]
+        if k < 2:
+            self.own[k + 1] = value
+            self.step(k + 1).start()
+        else:
+            self.tz[self.place.z] = value
+            each(1, self.place.depth, lambda k: self.along(k).start())
+
+    def along(self, k):
+        mine = self.tz.at[self.place.z]
+        return remote(
+            mine, mine, self.send.at[2 + k], self.recv.at[2 + k], self.place.device(0, self.place.turn(k))
+        )
+
+    def end(self):
+        each(1, self.place.depth, lambda k: self.along(k).wait())
+        total = self.tz[0]
+        for k in range(1, self.place.depth):
+            total = total + self.tz[k]
+        return total
+
+
 def compute_kernel(
-    fsdp, anch, dirs, delt, fore, cot, var, ng, nb, lg, lb, cg, cb, *rest
+    fsdp, rc, anch, dirs, delt, fore, cot, var, ng, nb, lg, lb, cg, cb, *rest
 ):
     layers, rest = rest[:18], rest[18:]
-    compute_body(fsdp, layers, anch, dirs, delt, fore, cot, var, ng, nb, lg, lb, cg, cb, *rest)
+    compute_body(fsdp, rc, layers, anch, dirs, delt, fore, cot, var, ng, nb, lg, lb, cg, cb, *rest)
 
 
 def compute_body(
-    fsdp, layers, anch, dirs, delt, fore, cot, var, ng, nb, lg, lb, cg, cb,
-    rgb_o, ag_o, dg_o, deltag_o, gout, tot_o, inv_o, smalls,
-    gathered, wid, send, recv, wts, sm, wt, w, wt7, w0t, w0, wcft, wcx, wclt, wcl, w7s, bb,
+    fsdp, RC, layers, anch, dirs, delt, fore, cot, var, ng, nb, lg, lb, cg, cb,
+    rgb_o, ag_o, dg_o, deltag_o, share_o, tot_o, inv_o, smalls,
+    gathered, wid, send, recv,
+    rcc, rca, rcb, rcz, rsend, sc, sa, sb, sz, tc, ta, tb, tz, town, tsend, trecv, wts, sm, wt, w, wt7, w0t, w0, wcft, wcx, wclt, wcl, w7s, bb,
     enc, fe, xt, dep, cols,
     hx, ss, us, zg, ts, fx, hc, dc, zc, encb, dzb,
     de, nr, row7, rowc, dzr, dx, eb, outc,
     acc, acc0, accx, accl, vac,
 ):
     rays = delt.shape[0]
+    PTS = RC * SAMP
+    NSUB = PTS // SUB
     lane128 = iota((1, 128), 1)
 
     place = Place(fsdp)
     barrier = pltpu.get_barrier_semaphore()
     place.greet(barrier)
-    gathered[place.index(0, place.z)] = own_share(*layers, wid)
+    for q, part in enumerate(own_share(*layers, wid)):
+        gathered[q, place.index(0, place.z)] = part
     place.wait_all(barrier)
 
     def meanwhile():
@@ -354,12 +497,12 @@
         ],
         axis=0,
     )
-    r = H // gathered.shape[0]
-    rp = gathered.shape[1] // GROUPS
-    for q in range(GROUPS // 2):
-        pair = gathered[:, 2 * rp * q : 2 * rp * (q + 1), :].astype(F32)
-        wts[2 * q] = pair[:, 0:r].reshape(H, H).astype(BF)
-        wts[2 * q + 1] = pair[:, rp : rp + r].reshape(H, H).astype(BF)
+    r = H // gathered.shape[1]
+    rp = gathered.shape[2] // 2
+    for q, groups in enumerate(PAIRS):
+        pair = gathered[q].astype(F32)
+        wts[groups[0]] = pair[:, 0:r].reshape(H, H).astype(BF)
+        wts[groups[1]] = pair[:, rp : rp + r].reshape(H, H).astype(BF)
 
     unit = (iota((H, H), 0) == iota((H, H), 1)).astype(BF)
 
@@ -410,9 +553,17 @@
 
     inv_s = jnp.exp(10.0 * smalls[6:7, 0:1])
 
-    def chunk(i, carry):
-        r0 = pl.multiple_of(i * RC, RC)
-        e0 = pl.multiple_of(i * (RC * EROWS), 8)
+    reduction = Reduction(place, gathered, share_o, rcc, rca, rcb, rcz, rsend, sc, sa, sb, sz)
+
+    def grad_of(k):
+        return turned(acc[k, 0:H].astype(BF))
+
+    def chunk(i, last):
+        if last:
+            r0, e0 = i * RC, i * RC * EROWS
+        else:
+            r0 = pl.multiple_of(i * RC, RC)
+            e0 = pl.multiple_of(i * (RC * EROWS), 8)
 
         def sub(j):
             return slice(j * SUB, (j + 1) * SUB)
@@ -487,8 +638,11 @@
         def feature(f):
             return fe[f, pl.ds(r0, RC), :]
 
-        dcol = [percol_ref_col(cols, r0, 3 + c) for c in range(3)]
-        ccol = [percol_ref_col(cols, r0, 6 + c) for c in range(3)]
+        def ray_col(j):
+            return jnp.broadcast_to(cols[pl.ds(r0, RC), j : j + 1], (RC, SAMP))
+
+        dcol = [ray_col(3 + c) for c in range(3)]
+        ccol = [ray_col(6 + c) for c in range(3)]
         normal = []
         for c in range(3):
             n = ray_row(de, c, EROWS)
@@ -570,12 +724,16 @@
         for l in range(3, 0, -1):
             zc[l - 1] = nn(w[5 + l], zc[l]).astype(BF) * dc[l - 1]
             acc[5 + l] += nt(hc[l - 1], zc[l])
+            if last and l == 2:
+                reduction.begin(0, grad_of(7), grad_of(8))
         dd = nn(wcx[...], zc[0]).astype(BF).astype(F32)
         for j in range(NSUB):
             spread_rows(dx, j, EROWS, dd[:, sub(j)])
         accx[...] += nt(fx[...], zc[0])
         accl[0] += nt(dzb[:, 0:PTS], hc[3, 0:H])
         fx[0:H] = nn(w[10], zc[0]).astype(BF)
+        if last:
+            reduction.begin(1, grad_of(6), turned(accx[0:H].astype(BF)))
 
         dpoint, dview = [], []
         for c in range(3):
@@ -622,6 +780,8 @@
                     x = ROOT_HALF * jnp.concatenate([g[0:EROWS] + e, g[EROWS:]], axis=0)
                     x = x.astype(BF)
                 hx[l, 0:H, sub2(j)] = x
+            if last and l in (3, 6):
+                reduction.step_a(0 if l == 3 else 1)
 
         dd = nn(w[9], fx[0:H])
         for j in range(NSUB):
@@ -640,7 +800,23 @@
                     d = d.astype(BF)
                 zg[l - 1, :, sub(j)] = d * ss[l - 1, :, sub(j)] + ts[l - 1, :, sub(j)]
             acc[l - 1] += nt(hx[l - 1], zg[l])
+            if last and l == 6:
+                reduction.begin(2, acc[9, 0:H], grad_of(5))
+                reduction.step_b(0)
+            elif last and l == 4:
+                reduction.begin(3, grad_of(4), grad_of(3))
+                reduction.step_a(2)
+                reduction.step_b(1)
+            elif last and l == 3:
+                reduction.step_z(0)
+            elif last and l == 2:
+                reduction.begin(4, acc[2, 0:H], grad_of(1))
+                reduction.step_a(3)
+                reduction.step_b(2)
+                reduction.step_z(1)
         acc0[...] += nt(encb[...], zg[0])
+        if last:
+            finish_weights()
         dd = nn(w0[...], zg[0, :, 0:PTS]).astype(BF).astype(F32)
         for j in range(NSUB):
             spread_rows(dx, j, EROWS, dd[:, sub(j)] + gather_rows(dx, 0, j, EROWS))
@@ -661,64 +837,78 @@
         outc[pl.ds(r0, RC), :] = out
         later = exact(ddepth, (iota((SAMP, SAMP), 0) >= iota((SAMP, SAMP), 1)).astype(F32))
         deltag_o[pl.ds(r0, RC), :] = ddelta + later - 0.5 * ddepth
-        return carry
-
-    lax.fori_loop(0, rays // RC, chunk, 0)
-
+
+    total = Total(place, tc, ta, tb, tz, town, tsend, trecv)
+
+    def finish_weights():
+        tail_rows = jnp.where(row8 == 0, accl[1, 0:8], accl[0, 0:8])
+        lines = [acc[0, H : H + 1]]
+        for k in (0, 1, 4, 5, 3, 0, 6, 7, 8):
+            lines.append(acc[k, H : H + 1])
+        small_rows = jnp.concatenate(lines, axis=0)
+        upper = jnp.concatenate(
+            [
+                acc0[...],
+                jnp.zeros((CROSS - EROWS, H), F32),
+                accx[H : H + EROWS],
+                jnp.zeros((BIASES - CROSS - EROWS, H), F32),
+                small_rows,
+                jnp.zeros((TAIL - BIASES - 10, H), F32),
+                tail_rows,
+                jnp.zeros((H - TAIL - 8, H), F32),
+            ],
+            axis=0,
+        )
+        packed = turned(upper.astype(BF))
+        reduction.begin(5, grad_of(0), packed)
+
+        def amount(k):
+            return jnp.sum(jnp.sum(vac[k], axis=1, keepdims=True), axis=0, keepdims=True)
+
+        lane_bias = jnp.zeros((1, H), F32)
+        for k in range(4):
+            lane_bias = lane_bias + jnp.where(lane256 == TAIL + k, amount(1 + k), 0.0)
+        variance = jnp.where(lane256 == 0, amount(0) * inv_s * 10.0, 0.0)
+        sums = jnp.concatenate(
+            [
+                jnp.sum(d3 * acc[2, 0:H], axis=0, keepdims=True),
+                acc[2, H : H + 1],
+                jnp.sum(d7 * acc[9, 0:H], axis=0, keepdims=True),
+                acc[9, H : H + 1],
+                jnp.sum(misc * packed, axis=0, keepdims=True),
+                lane_bias,
+                variance,
+                jnp.zeros((1, H), F32),
+            ],
+            axis=0,
+        )
+        total.begin(sums)
+
+    each(0, rays // RC - 1, lambda i: chunk(i, False))
+    chunk(rays // RC - 1, True)
+
+    reduction.step_a(4)
+    reduction.step_b(3)
+    reduction.step_z(2)
+    reduction.step_a(5)
+    total.go_on(0)
+    reduction.step_b(4)
+    reduction.step_z(3)
     result = outc[...].T
     rgb_o[...] = result[0:3, 0:rays]
     ag_o[...] = result[3:6, 0:rays]
     dg_o[...] = result[6:9, 0:rays]
-    tail_rows = jnp.where(row8 == 0, accl[1, 0:8], accl[0, 0:8])
-    lines = [acc[0, H : H + 1]]
-    for k in (0, 1, 4, 5, 3, 0, 6, 7, 8):
-        lines.append(acc[k, H : H + 1])
-    small_rows = jnp.concatenate(lines, axis=0)
-    upper = jnp.concatenate(
-        [
-            acc0[...],
-            jnp.zeros((CROSS - EROWS, H), F32),
-            accx[H : H + EROWS],
-            jnp.zeros((BIASES - CROSS - EROWS, H), F32),
-            small_rows,
-            jnp.zeros((TAIL - BIASES - 10, H), F32),
-            tail_rows,
-            jnp.zeros((H - TAIL - 8, H), F32),
-        ],
-        axis=0,
-    )
-    packed = turned(upper.astype(BF))
-    groups = [turned(acc[k, 0:H].astype(BF)) for k in (0, 1, 4, 5, 3, 6, 7, 8)]
-    groups += [turned(accx[0:H].astype(BF)), packed, acc[2, 0:H], acc[9, 0:H]]
-
-    for q in range(GROUPS // 2):
-        pair = [groups[2 * q + t].reshape(H // rp, rp, H) for t in range(2)]
-        gout[:, 2 * rp * q : 2 * rp * (q + 1), :] = jnp.concatenate(pair, axis=1).astype(BF)
-
-    def total(k):
-        return jnp.sum(jnp.sum(vac[k], axis=1, keepdims=True), axis=0, keepdims=True)
-
-    lane_bias = jnp.zeros((1, H), F32)
-    for k in range(4):
-        lane_bias = lane_bias + jnp.where(lane256 == TAIL + k, total(1 + k), 0.0)
-    variance = jnp.where(lane256 == 0, total(0) * inv_s * 10.0, 0.0)
-    tot_o[...] = jnp.concatenate(
-        [
-            jnp.sum(d3 * acc[2, 0:H], axis=0, keepdims=True),
-            acc[2, H : H + 1],
-            jnp.sum(d7 * acc[9, 0:H], axis=0, keepdims=True),
-            acc[9, H : H + 1],
-            jnp.sum(misc * packed, axis=0, keepdims=True),
-            lane_bias,
-            variance,
-            jnp.zeros((1, H), F32),
-        ],
-        axis=0,
-    )
-
-
-def percol_ref_col(ref, r0, j):
-    return jnp.broadcast_to(ref[pl.ds(r0, RC), j : j + 1], (RC, SAMP))
+    total.go_on(1)
+    reduction.step_b(5)
+    reduction.step_z(4)
+    total.go_on(2)
+    reduction.step_z(5)
+    for q in range(5):
+        reduction.step_end(q)
+    tot_o[...] = total.end()
+    reduction.step_end(5)
+    for q in range(6):
+        reduction.settle(q)
 
 
 def compute(fsdp, devices, anchors, directions, deltas, foreground, cotangent, smalls, layers):
@@ -726,11 +916,30 @@
     vm, dma = pltpu.VMEM, pltpu.SemaphoreType.DMA
     rp = layers[0].shape[0]
     points = rays * EROWS
+    RC = 8 if devices <= 32 else 4
+    PTS = RC * SAMP
+    depth = fsdp // 2
     scratch = [
-        vm((devices, GROUPS * rp, H), BF),
+        vm((6, devices, 2 * rp, H), BF),
         vm((4, rp, 384), F32),
         dma((2, devices)),
         dma((2, devices)),
+        vm((6, 2, 2 * depth, 2 * rp, H), BF),
+        vm((6, 2 * depth, 2 * rp, H), BF),
+        vm((6, depth, 2 * rp, H), BF),
+        vm((6, depth, 2 * rp, H), BF),
+        dma((6, 3 + depth)),
+        dma((6, 2)),
+        dma((6,)),
+        dma((6,)),
+        dma((6, depth)),
+        vm((8, H), F32),
+        vm((8, H), F32),
+        vm((8, H), F32),
+        vm((depth, 8, H), F32),
+        vm((3, 8, H), F32),
+        dma((2 + depth,)),
+        dma((2 + depth,)),
         vm((GROUPS, H, H), BF),
         vm((8, 384), F32),
         vm((9, H, H), BF),
@@ -779,14 +988,14 @@
         jax.ShapeDtypeStruct((3, rays), F32),
         jax.ShapeDtypeStruct((3, rays), F32),
         jax.ShapeDtypeStruct((rays, SAMP), F32),
-        jax.ShapeDtypeStruct((H // rp, GROUPS * rp, H), BF),
+        jax.ShapeDtypeStruct((GROUPS * rp, H), F32),
         jax.ShapeDtypeStruct((8, H), F32),
         jax.ShapeDtypeStruct((8, H), F32),
         jax.ShapeDtypeStruct((8, H), F32),
     )
     whole = pl.BlockSpec(memory_space=pltpu.VMEM)
     return pl.pallas_call(
-        functools.partial(compute_kernel, fsdp),
+        functools.partial(compute_kernel, fsdp, RC),
         out_shape=shapes,
         in_specs=[whole] * 30,
         out_specs=(whole,) * 8,
@@ -796,147 +1005,6 @@
             collective_id=0, has_side_effects=True, vmem_limit_bytes=62 * 1024 * 1024
         ),
     )(anchors, directions, deltas, foreground, cotangent, *smalls, *layers)
-
-
-def scatter_kernel(fsdp, g, tot, share, tot_o, rcc, rca, rcb, rcz, tc, ta, tb, tz, send, sc, sa, sb, sz, tsend, trecv):
-    place = Place(fsdp)
-    z, depth = place.z, place.depth
-    barrier = pltpu.get_barrier_semaphore()
-    place.greet(barrier)
-    place.wait_all(barrier)
-    rows = g.shape[1] // 2
-
-    def own(half, k, a, b, c):
-        return g.at[place.index(half, place.turn(k), a, b, c), pl.ds(half * rows, rows)]
-
-    def add(x, y):
-        return x[...].astype(F32) + y[...].astype(F32)
-
-    def to_core(half, k, a, b):
-        slot = k * 4 + a * 2 + b
-        return remote(
-            own(half, k, a, b, 1), rcc.at[half, slot], send.at[half, slot], sc.at[half, slot],
-            place.device(half, z, 0, 0, 1),
-        )
-
-    def to_a(half, k, b):
-        slot = k * 2 + b
-        return remote(
-            rcc.at[half, k * 4 + 2 + b], rca.at[half, slot], send.at[half, 4 * depth + slot],
-            sa.at[half, slot], place.device(half, z, 1),
-        )
-
-    def to_b(half, k):
-        return remote(
-            rca.at[half, k * 2 + 1], rcb.at[half, k], send.at[half, 6 * depth + k], sb.at[half, k],
-            place.device(half, z, 0, 1),
-        )
-
-    def to_z(half, k):
-        return remote(
-            rcb.at[half, k], rcz.at[half, k], send.at[half, 7 * depth + k], sz.at[half, k],
-            place.device(half, place.turn(k)),
-        )
-
-    def tot_copy(src, dst, k, *to):
-        return remote(src, dst, tsend.at[k], trecv.at[k], place.device(0, *to))
-
-    def order(body):
-        each(1, depth, body)
-        body(0)
-
-    t_core = tot_copy(tot, tc, 0, z, 0, 0, 1)
-    t_core.start()
-    for a, b in ((1, 1), (1, 0), (0, 1), (0, 0)):
-
-        def start_core(k):
-            for half in range(2):
-                to_core(half, k, a, b).start()
-
-        order(start_core)
-
-    def join_core(k, a, b):
-        for half in range(2):
-            slot = k * 4 + a * 2 + b
-            to_core(half, k, a, b).wait_recv()
-            rcc[half, slot] = add(rcc.at[half, slot], own(half, k, a, b, 0)).astype(BF)
-            if a:
-                to_a(half, k, b).start()
-
-    order(lambda k: join_core(k, 1, 1))
-    order(lambda k: join_core(k, 1, 0))
-    t_core.wait()
-    tc[...] = tot[...] + tc[...]
-    t_a = tot_copy(tc, ta, 1, z, 1)
-    t_a.start()
-    order(lambda k: join_core(k, 0, 1))
-    order(lambda k: join_core(k, 0, 0))
-    t_a.wait()
-    ta[...] = tc[...] + ta[...]
-    t_b = tot_copy(ta, tb, 2, z, 0, 1)
-    t_b.start()
-
-    def join_a(k, b):
-        for half in range(2):
-            slot = k * 2 + b
-            to_a(half, k, b).wait_recv()
-            rca[half, slot] = add(rca.at[half, slot], rcc.at[half, k * 4 + b]).astype(BF)
-            if b:
-                to_b(half, k).start()
-
-    order(lambda k: join_a(k, 1))
-    t_b.wait()
-    tz[z] = ta[...] + tb[...]
-
-    def start_tot(k):
-        tot_copy(tz.at[z], tz.at[z], 2 + k, place.turn(k)).start()
-
-    each(1, depth, start_tot)
-    order(lambda k: join_a(k, 0))
-
-    def join_b(k):
-        for half in range(2):
-            to_b(half, k).wait_recv()
-            rcb[half, k] = add(rcb.at[half, k], rca.at[half, k * 2]).astype(BF)
-            to_z(half, k).start()
-
-    each(1, depth, join_b)
-    for half in range(2):
-        to_b(half, 0).wait_recv()
-        share[half * rows : (half + 1) * rows] = add(rcb.at[half, 0], rca.at[half, 0])
-
-    def join_z(k):
-        for half in range(2):
-            to_z(half, k).wait_recv()
-            share[half * rows : (half + 1) * rows] += rcz[half, k].astype(F32)
-
-    each(1, depth, join_z)
-
-    def end_tot(k):
-        tot_copy(tz.at[z], tz.at[z], 2 + k, place.turn(k)).wait()
-
-    each(1, depth, end_tot)
-    total = tz[0]
-    for k in range(1, depth):
-        total = total + tz[k]
-    tot_o[...] = total
-
-    def sent(k):
-        for half in range(2):
-            for a in range(2):
-                for b in range(2):
-                    to_core(half, k, a, b).wait_send()
-            to_a(half, k, 0).wait_send()
-            to_a(half, k, 1).wait_send()
-            to_b(half, k).wait_send()
-
-    each(0, depth, sent)
-
-    def sent_z(k):
-        for half in range(2):
-            to_z(half, k).wait_send()
-
-    each(1, depth, sent_z)
 
 
 def unscaled_rows(d, gain, grad):
@@ -961,7 +1029,8 @@
         return column(as_row(ref) if k is None else ref[...].astype(F32)[k : k + 1])
 
     def group(k):
-        return share[k * r : (k + 1) * r, :]
+        at = [g for pair in PAIRS for g in pair].index(k)
+        return share[at * r : (at + 1) * r, :]
 
     def put(ref, col):
         ref[...] = line(col).reshape(r)
@@ -1050,9 +1119,7 @@
 ):
     r = sdf_first_gain.shape[0]
     rp = max(r, 8)
-    depth = fsdp // 2
     whole = pl.BlockSpec(memory_space=pltpu.VMEM)
-    vm, dma = pltpu.VMEM, pltpu.SemaphoreType.DMA
 
     def rows(x):
         return x if rp == r else jnp.pad(x, [(0, 0)] * (x.ndim - 2) + [(0, rp - r), (0, 0)])
@@ -1076,17 +1143,7 @@
             color_first_gain, color_first_bias, color_mid_gain, color_mid_bias, color_last_dir.T,
         )
     )
-    size = GROUPS * rp
-    limit = 60 * 1024 * 1024
-    blocks = H // rp
-
-    def ungroup(x):
-        if rp == r:
-            return x
-        x = x.reshape(blocks, GROUPS, devices // blocks, r, H).transpose(0, 2, 1, 3, 4)
-        return rows(x).reshape(devices, size, H)
-
-    rgb, ag, dg, deltag, gout, tot, inv, smalls = compute(
+    rgb, ag, dg, deltag, share, tot, inv, smalls = compute(
         fsdp, devices, anchors, directions, deltas, foreground, rgb_cotangent,
         (
             variance, sdf_narrow_gain, sdf_narrow_bias, sdf_last_gain, sdf_last_bias,
@@ -1094,35 +1151,6 @@
         ),
         (*shares, fg, fb, mg, mb, sg, sb, cg, cb, cmg, cmb, cl),
     )
-    half = size // 2
-    share, tot = pl.pallas_call(
-        functools.partial(scatter_kernel, fsdp),
-        out_shape=(jax.ShapeDtypeStruct((size, H), F32), jax.ShapeDtypeStruct((8, H), F32)),
-        in_specs=[whole] * 2,
-        out_specs=(whole,) * 2,
-        scratch_shapes=[
-            vm((2, 4 * depth, half, H), BF),
-            vm((2, 2 * depth, half, H), BF),
-            vm((2, depth, half, H), BF),
-            vm((2, depth, half, H), BF),
-            vm((8, H), F32),
-            vm((8, H), F32),
-            vm((8, H), F32),
-            vm((depth, 8, H), F32),
-            dma((2, 8 * depth)),
-            dma((2, 4 * depth)),
-            dma((2, 2 * depth)),
-            dma((2, depth)),
-            dma((2, depth)),
-            dma((2 + depth,)),
-            dma((2 + depth,)),
-        ],
-        name="scatter",
-        compiler_params=pltpu.CompilerParams(
-            collective_id=1, has_side_effects=True, vmem_limit_bytes=limit
-        ),
-    )(ungroup(gout), tot)
-
     def f32(*shape):
         return jax.ShapeDtypeStruct(shape, F32)
 
@@ -1142,7 +1170,7 @@
         ),
         in_specs=[whole] * 21,
         out_specs=(whole,) * 29,
-        scratch_shapes=[vm((4, rp, 384), F32)],
+        scratch_shapes=[pltpu.VMEM((4, rp, 384), F32)],
         name="finish",
     )(share, tot, inv, smalls, *shares, fg, mg, sg, cg, cmg, cl, rgb, ag, dg, deltag)
     (

time: 99.6 us -> 99.2 us (level)
    pallas_call x2 -> x1, Pallas kernels: 95.7 us -> 95.3 us  [compute(): pl.pallas_call(functools.partial(compute_kernel, fsdp, RC), out_shape=sha...]
where the time goes in v2:
time: 99.2 us; the launch traced here: 99 us
  Pallas kernels  97.5 us (98%)
  between operations  1.53 us (2%)
    pallas_call x1, Pallas kernels, compute(): pl.pallas_call(functools.partial(compute_kernel, fsdp, RC), out_shape=sha...  95.3 us
    pallas_call x1, Pallas kernels, per_device(): pl.pallas_call(finish_kernel, out_shape=(f32(*rgb.shape), f32(*ag.shape),...  2.2 us

profile of v2, /device:TPU:0, one launch (start us, length us, event | category | flops | bytes accessed | tf_op | source)
XLA Modules:
  0.0 99.0 jit_solution(16473997199142484108)
XLA Ops:
  1.3 95.3 %nets.1 = (f32[3,32]{1,0:T(4,128)}, f32[3,32]{1,0:T(4,128)}, f32[3,32]{1,0:T(4,128)}, f32[32,128]{1,0:T(8,128)}, f32[96,256]{1,0:T(8,128)}, /*index=5*/f32[8,256...) custom-call(f32[3,32]{1,0:T(4,128)} %anch.1, f32[3,32]{1,0:T(4,128)} %dirs.1, f32[32,128]{1,0:T(8,128)} %delt.1, s32[32,128]{1,0:T(8,128)} %fore.1, ...), custom_call_target="tpu_custom_call" | custom-call | tf_op jit(solution)/shard_map/nets/pallas_call | solution.py:997
  96.6 2.2 %finish.1 = (f32[3,32]{1,0:T(4,128)}, f32[3,32]{1,0:T(4,128)}, f32[3,32]{1,0:T(4,128)}, f32[32,128]{1,0:T(8,128)}, f32[8,39]{1,0:T(8,128)}, /*index=5*/f32[8]{0:...) custom-call(f32[96,256]{1,0:T(8,128)} %get-tuple-element.66.share, ...), custom_call_target="tpu_custom_call" | custom-call | tf_op jit(solution)/shard_map/finish/pallas_call | solution.py:1157

commit v3 on v2

--- a/solution.py
+++ b/solution.py
@@ -22,6 +22,7 @@
 CROSS = 128
 BIASES = 200
 TAIL = 216
+TOT = 24
 EPS = 1e-06
 HALF_LN2 = 0.34657359027997264
 ROOT_HALF = 0.7071067811865476
@@ -64,13 +65,11 @@
 
 
 def sharp(z):
-    z = z.astype(BF)
     s = 0.5 * jnp.tanh(z) + 0.5
     return jnp.maximum(z, 0.0) - 0.5 * jnp.log(jnp.maximum(s, 1.0 - s)), s
 
 
 def silu(z):
-    z = z.astype(BF)
     g = 0.5 * jnp.tanh(0.5 * z) + 0.5
     h = z * g
     return h, g + h * (1.0 - g)
@@ -603,7 +602,7 @@
                 if l > 0:
                     z = z + wide(bb[l - 1])
                 h, s = sharp(z)
-                ss[l, :, sub(j)] = s.astype(BF)
+                ss[l, :, sub(j)] = s
                 if l == 3:
                     e = gather_rows(enc, e0, j, EROWS)
                     keep = iota((EROWS, 1), 0) < ENC
@@ -619,17 +618,16 @@
             spread_rows(row7, j, 16, z[H : H + 16])
 
         for j in range(NSUB):
-            zg[6, :, sub2(j)] = wide(w7s[...]).astype(BF) * ss[6, :, sub(j)]
+            zg[6, :, sub2(j)] = (wide(w7s[...]) * ss[6, :, sub(j)]).astype(BF)
         for l in range(6, 0, -1):
             uu = nn(w[l - 1], zg[l, :, PTS:])
             for j in range(NSUB):
-                u = uu[:, sub(j)].astype(BF)
+                u = uu[:, sub(j)].astype(BF).astype(F32)
                 if l == 4:
-                    u = u.astype(F32) * ROOT_HALF
+                    u = u * ROOT_HALF
                     spread_rows(de, j, EROWS, u)
-                    u = u.astype(BF)
-                us[l - 1, :, sub(j)] = u
-                zg[l - 1, :, sub2(j)] = u * ss[l - 1, :, sub(j)]
+                us[l - 1, :, sub(j)] = u.astype(BF)
+                zg[l - 1, :, sub2(j)] = (u * ss[l - 1, :, sub(j)]).astype(BF)
         dd = nn(w0[...], zg[0, :, PTS:]).astype(BF).astype(F32)
         for j in range(NSUB):
             d = dd[:, sub(j)]
@@ -769,10 +767,11 @@
                 g = gg[:, sub(j)]
                 s = ss[l, :, sub(j)]
                 if l == 3:
-                    g = g * s.astype(F32)
+                    g = g * s
                     x = g.astype(BF)
                 else:
-                    x = g.astype(BF) * s
+                    x = (g * s).astype(BF)
+                s = s.astype(BF)
                 u = wide(w7s[...]).astype(BF) if l == 6 else us[l, :, sub(j)]
                 ts[l, :, sub(j)] = x * u * (2.0 - 2.0 * s)
                 if l == 3:
@@ -780,14 +779,14 @@
                     x = ROOT_HALF * jnp.concatenate([g[0:EROWS] + e, g[EROWS:]], axis=0)
                     x = x.astype(BF)
                 hx[l, 0:H, sub2(j)] = x
-            if last and l in (3, 6):
-                reduction.step_a(0 if l == 3 else 1)
+            if last and l == 6:
+                reduction.step_a(0)
 
         dd = nn(w[9], fx[0:H])
         for j in range(NSUB):
             row = gather_rows(dzr, 0, j, 16)[0:1]
             d = dd[:, sub(j)] + wide(w7s[...]) * row
-            zg[6, :, sub(j)] = d.astype(BF) * ss[6, :, sub(j)] + ts[6, :, sub(j)]
+            zg[6, :, sub(j)] = d.astype(BF) * ss[6, :, sub(j)].astype(BF) + ts[6, :, sub(j)]
         acc[9] += nt(hx[6, :, 0:PTS], fx[0:H])
         accl[1] += nt(dzb[...], hx[6, 0:H])
         for l in range(6, 0, -1):
@@ -798,22 +797,18 @@
                     d = d.astype(F32) * ROOT_HALF
                     spread_rows(dx, j, EROWS, d)
                     d = d.astype(BF)
-                zg[l - 1, :, sub(j)] = d * ss[l - 1, :, sub(j)] + ts[l - 1, :, sub(j)]
+                zg[l - 1, :, sub(j)] = d * ss[l - 1, :, sub(j)].astype(BF) + ts[l - 1, :, sub(j)]
             acc[l - 1] += nt(hx[l - 1], zg[l])
             if last and l == 6:
                 reduction.begin(2, acc[9, 0:H], grad_of(5))
-                reduction.step_b(0)
+                reduction.step_a(1)
             elif last and l == 4:
                 reduction.begin(3, grad_of(4), grad_of(3))
+            elif last and l == 3:
                 reduction.step_a(2)
-                reduction.step_b(1)
-            elif last and l == 3:
-                reduction.step_z(0)
+                reduction.step_b(0)
             elif last and l == 2:
                 reduction.begin(4, acc[2, 0:H], grad_of(1))
-                reduction.step_a(3)
-                reduction.step_b(2)
-                reduction.step_z(1)
         acc0[...] += nt(encb[...], zg[0])
         if last:
             finish_weights()
@@ -879,6 +874,11 @@
                 lane_bias,
                 variance,
                 jnp.zeros((1, H), F32),
+            acc0[ENC : ENC + 1],
+            *lines[1:6],
+            accx[H + NX : H + NX + 1],
+            *lines[7:],
+            jnp.zeros((TOT - 18, H), F32),
             ],
             axis=0,
         )
@@ -887,22 +887,26 @@
     each(0, rays // RC - 1, lambda i: chunk(i, False))
     chunk(rays // RC - 1, True)
 
+    reduction.step_a(3)
+    reduction.step_b(1)
     reduction.step_a(4)
+    total.go_on(0)
+    reduction.step_a(5)
+    reduction.step_b(2)
+    reduction.step_z(0)
     reduction.step_b(3)
+    total.go_on(1)
+    reduction.step_z(1)
+    reduction.step_b(4)
     reduction.step_z(2)
-    reduction.step_a(5)
-    total.go_on(0)
-    reduction.step_b(4)
-    reduction.step_z(3)
+    reduction.step_b(5)
+    total.go_on(2)
     result = outc[...].T
     rgb_o[...] = result[0:3, 0:rays]
     ag_o[...] = result[3:6, 0:rays]
     dg_o[...] = result[6:9, 0:rays]
-    total.go_on(1)
-    reduction.step_b(5)
-    reduction.step_z(4)
-    total.go_on(2)
-    reduction.step_z(5)
+    for q in range(3, 6):
+        reduction.step_z(q)
     for q in range(5):
         reduction.step_end(q)
     tot_o[...] = total.end()
@@ -933,11 +937,11 @@
         dma((6,)),
         dma((6,)),
         dma((6, depth)),
-        vm((8, H), F32),
-        vm((8, H), F32),
-        vm((8, H), F32),
-        vm((depth, 8, H), F32),
-        vm((3, 8, H), F32),
+        vm((TOT, H), F32),
+        vm((TOT, H), F32),
+        vm((TOT, H), F32),
+        vm((depth, TOT, H), F32),
+        vm((3, TOT, H), F32),
         dma((2 + depth,)),
         dma((2 + depth,)),
         vm((GROUPS, H, H), BF),
@@ -959,7 +963,7 @@
         vm((rays, SAMP), F32),
         vm((128, 128), F32),
         vm((7, H + 16, 2 * PTS), BF),
-        vm((7, H, PTS), BF),
+        vm((7, H, PTS), F32),
         vm((6, H, PTS), BF),
         vm((7, H, 2 * PTS), BF),
         vm((7, H, PTS), BF),
@@ -989,7 +993,7 @@
         jax.ShapeDtypeStruct((3, rays), F32),
         jax.ShapeDtypeStruct((rays, SAMP), F32),
         jax.ShapeDtypeStruct((GROUPS * rp, H), F32),
-        jax.ShapeDtypeStruct((8, H), F32),
+        jax.ShapeDtypeStruct((TOT, H), F32),
         jax.ShapeDtypeStruct((8, H), F32),
         jax.ShapeDtypeStruct((8, H), F32),
     )
@@ -1014,7 +1018,7 @@
 
 
 def finish_kernel(
-    share, tot, inv, smalls, first, mid, narrow, skip, last, cfirst, cmid,
+    real, share, tot, inv, smalls, first, mid, narrow, skip, last, cfirst, cmid,
     fg, mg, sg, cg, cmg, cl, rgb, ag, dg, deltag, o_rgb, o_ag, o_dg, o_deltag,
     o_first, o_fg, o_fb, o_mid, o_mg, o_mb, o_narrow, o_ng, o_nb, o_skip, o_sg, o_sb,
     o_last, o_lg, o_lb, o_cfirst, o_cg, o_cb, o_cmid, o_cmg, o_cmb, o_clast, o_clg, o_clb, o_var,
@@ -1038,37 +1042,43 @@
     def put_rows(ref, columns):
         ref[...] = jnp.concatenate([line(col) for col in columns], axis=0)
 
+    first_unit = (lax.axis_index("fsdp") * 4 + lax.axis_index("rep")) * real
+    mine = iota((r, H), 1) == first_unit + iota((r, H), 0)
+
+    def bias(j):
+        return jnp.sum(jnp.where(mine, tot[8 + j : 9 + j, :], 0.0), axis=1, keepdims=True)
+
     misc = group(9)
     lane = iota((1, 128), 1)
     g, gain = unscaled_rows(d_first, vec(fg), jnp.where(lane < ENC, misc[:, 0:128], 0.0))
     o_first[...] = g[:, 0:ENC]
     put(o_fg, gain)
-    put(o_fb, misc[:, ENC : ENC + 1])
+    put(o_fb, bias(0))
     gains = []
     for k in range(4):
         g, gain = unscaled_rows(mid[k].astype(F32), vec(mg, k), group(k))
         o_mid[k] = g
         gains.append(gain)
     put_rows(o_mg, gains)
-    put_rows(o_mb, [misc[:, BIASES + 1 + k : BIASES + 2 + k] for k in range(4)])
+    put_rows(o_mb, [bias(1 + k) for k in range(4)])
     g, gain = unscaled_rows(skip[...].astype(F32), vec(sg), pltpu.roll(group(4), H - ENC, 1))
     o_skip[...] = g
     put(o_sg, gain)
-    put(o_sb, misc[:, BIASES + 5 : BIASES + 6])
+    put(o_sb, bias(5))
     extra = jnp.where(lane < NX, misc[:, 128:256], 0.0)
     moved = jnp.concatenate([group(8), jnp.zeros((r, 128), F32)], axis=1)
     grad = pltpu.roll(moved, NX, 1) + jnp.concatenate([extra, jnp.zeros((r, H), F32)], axis=1)
     g, gain = unscaled_rows(d_cfirst, vec(cg), grad)
     o_cfirst[...] = g[:, 0 : H + NX]
     put(o_cg, gain)
-    put(o_cb, misc[:, CROSS + NX : CROSS + NX + 1])
+    put(o_cb, bias(6))
     gains = []
     for k in range(3):
         g, gain = unscaled_rows(cmid[k].astype(F32), vec(cmg, k), group(5 + k))
         o_cmid[k] = g
         gains.append(gain)
     put_rows(o_cmg, gains)
-    put_rows(o_cmb, [misc[:, BIASES + 7 + k : BIASES + 8 + k] for k in range(3)])
+    put_rows(o_cmb, [bias(7 + k) for k in range(3)])
 
     def across(k, d, grad):
         gain, iv, dot = smalls[k : k + 1, :], inv[k : k + 1, :], tot[k : k + 1, :]
@@ -1090,7 +1100,7 @@
 
     o_last[...] = behind(g, t[:, TAIL : TAIL + 1])
     put_rows(o_clast, [t[:, TAIL + 1 + c : TAIL + 2 + c] for c in range(3)])
-    gained = tot[...] * inv[...]
+    gained = tot[0:8, :] * inv[...]
     back = pltpu.roll(jnp.concatenate([gained[0:1], tot[1:2], jnp.zeros((6, H), F32)], axis=0), H - ENC, 1)
     o_ng[...] = back[0:1, 0:NARROW].reshape(NARROW)
     o_nb[...] = back[1:2, 0:NARROW].reshape(NARROW)
@@ -1155,7 +1165,7 @@
         return jax.ShapeDtypeStruct(shape, F32)
 
     outs = pl.pallas_call(
-        finish_kernel,
+        functools.partial(finish_kernel, r),
         out_shape=(
             f32(*rgb.shape), f32(*ag.shape), f32(*dg.shape), f32(*deltag.shape),
             f32(rp, ENC), f32(rp), f32(rp),

time: 99.2 us -> 103 us (1.038)
  Pallas kernels: 97.5 us -> 102 us
    pallas_call x1, Pallas kernels: 95.3 us -> 99.6 us  [compute(): pl.pallas_call(functools.partial(compute_kernel, fsdp, RC), out_shape=sha...]
where the time goes in v3:
time: 103 us
  Pallas kernels  102 us (99%)
  between operations  1.53 us (1%)
    pallas_call x1, Pallas kernels, compute(): pl.pallas_call(functools.partial(compute_kernel, fsdp, RC), out_shape=sha...  99.6 us
    pallas_call x1, Pallas kernels, per_device(): pl.pallas_call(functools.partial(finish_kernel, r), out_shape=(f32(*rgb.s...  2.1 us

profile of v3, /device:TPU:0, one launch (start us, length us, event | category | flops | bytes accessed | tf_op | source)
XLA Modules:
  0.0 103.2 jit_solution(13291482696438391881)
XLA Ops:
  1.3 99.6 %nets.1 = (f32[3,32]{1,0:T(4,128)}, f32[3,32]{1,0:T(4,128)}, f32[3,32]{1,0:T(4,128)}, f32[32,128]{1,0:T(8,128)}, f32[96,256]{1,0:T(8,128)}, /*index=5*/f32[24,25...) custom-call(f32[3,32]{1,0:T(4,128)} %anch.1, f32[3,32]{1,0:T(4,128)} %dirs.1, f32[32,128]{1,0:T(8,128)} %delt.1, ...), custom_call_target="tpu_custom_call" | custom-call | tf_op jit(solution)/shard_map/nets/pallas_call | solution.py:1001
  100.9 2.1 %finish.1 = (f32[3,32]{1,0:T(4,128)}, f32[3,32]{1,0:T(4,128)}, f32[3,32]{1,0:T(4,128)}, f32[32,128]{1,0:T(8,128)}, f32[8,39]{1,0:T(8,128)}, /*index=5*/f32[8]{0:...) custom-call(f32[96,256]{1,0:T(8,128)} %get-tuple-element.66.share, ...), custom_call_target="tpu_custom_call" | custom-call | tf_op jit(solution)/shard_map/finish/pallas_call | solution.py:1167
